TPU v7x, 32 devices: a whole 2x2x4 slice. The times are simulated.
32 devices in a mesh: branch: 2 (over core), seq: 16 (over z, y, x).
Axes of the slice: x: 2, y: 2, z: 4, core: 2. Of those that a mesh axis runs over, the one named last changes fastest.
Arguments:
- hidden: bfloat16 [2, 12288, 1024], P('branch', 'seq')
- noisy_mel_state: float32 [100, 12288], P(None, 'seq'), may hold values from -6 to 6
- modulation: float32 [5, 1024], replicated, may hold values from -3 to 3
- feedforward_in_weight: bfloat16 [1024, 2048], replicated, may hold values from -0.1875 to 0.1875
- feedforward_in_bias: float32 [2048], replicated, may hold values from -1.75 to 1.75
- feedforward_out_weight: bfloat16 [2048, 1024], replicated, may hold values from -0.125 to 0.125
- feedforward_out_bias: float32 [1024], replicated, may hold values from -1.75 to 1.75
- mel_velocity_weight: bfloat16 [1024, 100], replicated, may hold values from -0.1875 to 0.1875
- mel_velocity_bias: float32 [100], replicated, may hold values from -3 to 3
- input_conv_weight: bfloat16 [700, 512], replicated, may hold values from -0.21875 to 0.21875
- input_conv_bias: float32 [512], replicated, may hold values from -1.75 to 1.75
- transposed_conv_weight: bfloat16 [4096, 512], replicated, may hold values from -0.1875 to 0.1875
- transposed_conv_bias: float32 [256], replicated, may hold values from -1.75 to 1.75
- snake_freq_first: float32 [256], replicated, may hold values from 0.5 to 3
- dilated_conv_weight: bfloat16 [768, 256], replicated, may hold values from -0.21875 to 0.21875
- dilated_conv_bias: float32 [256], replicated, may hold values from -1.75 to 1.75
- snake_freq_second: float32 [256], replicated, may hold values from 0.5 to 3
- second_conv_weight: bfloat16 [768, 256], replicated, may hold values from -0.21875 to 0.21875
- second_conv_bias: float32 [256], replicated, may hold values from -1.75 to 1.75
- frame_holder: int32 [12288], P('seq'), may hold values from 0 to 31, as said below
- frame_position: int32 [12288], P('seq'), may hold values from 0 to 767, as said below
- holder_utterance_length: int32 [32], replicated, may hold values from 1 to 768, as said below
Outputs:
- wave: bfloat16 [32, 256, 6144], P(('branch', 'seq'))
Inputs may be any that keep to these rules, and one draw needn't show every extreme that they name: `frame_holder`: the frames form 32 utterances, each a run of consecutive frames; all frames of an utterance name one owner, and each owner is named by exactly one utterance. `frame_position`: A frame's position in its utterance, 0 at the utterance's first frame. `holder_utterance_length`: the number of frames that name the owner; every utterance has at least one frame.
All inputs are finite; a program needn't handle non-finite values.
Results may differ from a plain program's by a relative error of at most 0.015.
Values may be sent and summed in bfloat16 or wider, within the bound.
A program may use at most 128 MiB of HBM per device.

v0:
```python
import math

import jax
import jax.numpy as jnp
from jax import lax
from jax.sharding import PartitionSpec as P

UP = 8
KT = 16
KPRE = 7
DILATION_RATE = 3
NFE = 16


GUIDE = 2.0


def partner(block, axis, distance):
    count = lax.axis_size(axis)
    route = []
    for low in range(count):
        high = low | 1 << distance
        if high != low and high < count:
            route += [(low, high), (high, low)]
    return lax.ppermute(block, axis, route)


def layer_norm(row_block):
    row_mean = jnp.mean(row_block, axis=-1, keepdims=True)
    centred = row_block - row_mean
    row_var = jnp.mean(centred * centred, axis=-1, keepdims=True)
    return centred * lax.rsqrt(row_var + 1e-06)


def velocity(
    row_block,
    modulation,
    feedforward_in_weight,
    feedforward_in_bias,
    feedforward_out_weight,
    feedforward_out_bias,
    mel_velocity_weight,
    mel_velocity_bias,
):
    residual_in = row_block.astype(jnp.float32)
    normed = (layer_norm(residual_in) * (1.0 + modulation[1]) + modulation[0]).astype(jnp.bfloat16)
    inner_pre = (
        jnp.dot(normed, feedforward_in_weight, preferred_element_type=jnp.float32)
        + feedforward_in_bias
    )
    active = jax.nn.gelu(inner_pre, approximate=True).astype(jnp.bfloat16)
    back_proj = (
        jnp.dot(active, feedforward_out_weight, preferred_element_type=jnp.float32)
        + feedforward_out_bias
    )
    block_out = residual_in + modulation[2] * back_proj
    final_norm = (layer_norm(block_out) * (1.0 + modulation[4]) + modulation[3]).astype(
        jnp.bfloat16
    )
    speed = lax.dot_general(
        mel_velocity_weight,
        final_norm,
        (((0,), (1,)), ((), ())),
        preferred_element_type=jnp.float32,
    )
    return speed + mel_velocity_bias[:, None]


def shifted(values, offset):
    pad_width = abs(offset)
    last_axis = values.ndim - 1
    pad_spec = [(0, 0)] * last_axis + [(pad_width, pad_width)]
    padded = jnp.pad(values, pad_spec)
    return lax.slice_in_dim(
        padded, pad_width + offset, pad_width + offset + values.shape[last_axis], axis=last_axis
    )


def snake(signal, alpha_vec):
    sine_part = jnp.sin(alpha_vec[:, None] * signal)
    return signal + sine_part * sine_part / alpha_vec[:, None]


def dilated_output(values, weight, bias_vec, spacing, keep_mask):
    stacked = jnp.concatenate([shifted(values, -spacing), values, shifted(values, spacing)], axis=0)
    conv_out = lax.dot_general(
        weight, stacked, (((0,), (0,)), ((), ())), preferred_element_type=jnp.float32
    )
    return jnp.where(keep_mask[None, :], conv_out + bias_vec[:, None], 0.0)


def vocoder_synthesize(
    holder_mel,
    utterance_frames_length,
    input_conv_weight,
    input_conv_bias,
    transposed_conv_weight,
    transposed_conv_bias,
    snake_freq_first,
    dilated_conv_weight,
    dilated_conv_bias,
    snake_freq_second,
    second_conv_weight,
    second_conv_bias,
):
    most_rows = holder_mel.shape[1]
    channels = transposed_conv_weight.shape[0] // KT
    frame_keep = jnp.arange(most_rows) < utterance_frames_length
    half_kernel = KPRE // 2
    tap_list = [shifted(holder_mel, tap_index - half_kernel) for tap_index in range(KPRE)]
    stacked = jnp.concatenate(tap_list, axis=0)
    pre_out = lax.dot_general(
        input_conv_weight, stacked, (((0,), (0,)), ((), ())), preferred_element_type=jnp.float32
    )
    pre_out = jnp.where(frame_keep[None, :], pre_out + input_conv_bias[:, None], 0.0).astype(
        jnp.bfloat16
    )
    phases = jnp.dot(transposed_conv_weight, pre_out, preferred_element_type=jnp.float32).reshape(
        KT, channels, most_rows
    )
    pad_up = UP // 2
    direct = phases[pad_up : pad_up + UP]
    early_part = shifted(phases[UP + pad_up :], -1)
    late_part = shifted(phases[: UP - pad_up], 1)
    phase_sum = direct + jnp.concatenate([early_part, late_part], axis=0)
    woven_out = (
        jnp.transpose(phase_sum, (1, 2, 0)).reshape(channels, most_rows * UP)
        + transposed_conv_bias[:, None]
    )
    sample_keep_mask = jnp.arange(most_rows * UP) < utterance_frames_length * UP
    upsampled = jnp.where(sample_keep_mask[None, :], woven_out, 0.0).astype(jnp.bfloat16)
    first_snake_output = snake(upsampled.astype(jnp.float32), snake_freq_first).astype(jnp.bfloat16)
    inner_convolved = dilated_output(
        first_snake_output, dilated_conv_weight, dilated_conv_bias, DILATION_RATE, sample_keep_mask
    )
    second_act = snake(inner_convolved, snake_freq_second).astype(jnp.bfloat16)
    outer_conv = dilated_output(
        second_act, second_conv_weight, second_conv_bias, 1, sample_keep_mask
    )
    return (upsampled.astype(jnp.float32) + outer_conv).astype(jnp.bfloat16)


def slot_table(slot_ids, slot_count):
    return (slot_ids[:, None] == jnp.arange(slot_count, dtype=jnp.int32)[None, :]).astype(
        jnp.bfloat16
    )


def local(
    hidden,
    noisy_mel_state,
    modulation,
    feedforward_in_weight,
    feedforward_in_bias,
    feedforward_out_weight,
    feedforward_out_bias,
    mel_velocity_weight,
    mel_velocity_bias,
    input_conv_weight,
    input_conv_bias,
    transposed_conv_weight,
    transposed_conv_bias,
    snake_freq_first,
    dilated_conv_weight,
    dilated_conv_bias,
    snake_freq_second,
    second_conv_weight,
    second_conv_bias,
    frame_holder,
    frame_position,
    holder_utterance_length,
):
    step_size = math.cos(0.5 * math.pi * (NFE - 1) / NFE)
    own_velocity = velocity(
        hidden[0],
        modulation,
        feedforward_in_weight,
        feedforward_in_bias,
        feedforward_out_weight,
        feedforward_out_bias,
        mel_velocity_weight,
        mel_velocity_bias,
    )
    mel_bins = own_velocity.shape[0]
    frame_count = own_velocity.shape[1]
    half_rows = frame_count // 2
    branch_side = lax.axis_index("branch")
    own_half = lax.dynamic_slice_in_dim(own_velocity, branch_side * half_rows, half_rows, 1)
    peer_full = partner(own_velocity, "branch", 0)
    peer_half = lax.dynamic_slice_in_dim(peer_full, branch_side * half_rows, half_rows, 1)
    conditional = jnp.where(branch_side == 0, own_half, peer_half)
    unconditional = jnp.where(branch_side == 0, peer_half, own_half)
    guided = (1.0 + GUIDE) * conditional - GUIDE * unconditional
    noisy_half = lax.dynamic_slice_in_dim(noisy_mel_state, branch_side * half_rows, half_rows, 1)
    refined = (noisy_half + step_size * guided).astype(jnp.bfloat16)
    owner_half = lax.dynamic_slice_in_dim(frame_holder, branch_side * half_rows, half_rows, 0)
    offset_half = lax.dynamic_slice_in_dim(frame_position, branch_side * half_rows, half_rows, 0)
    frame_tags = jnp.stack([owner_half, offset_half], axis=0)
    self_owner = lax.axis_index(("branch", "seq"))
    values = lax.all_gather(refined, ("branch", "seq"), axis=1, tiled=True)
    tag_rows = lax.all_gather(frame_tags, ("branch", "seq"), axis=1, tiled=True)
    piece_rows = values.shape[1]
    block_rows = math.gcd(piece_rows, 512)

    def add_block(block_index, total):
        block_values = lax.dynamic_slice_in_dim(values, block_index * block_rows, block_rows, 1)
        block_tags = lax.dynamic_slice_in_dim(tag_rows, block_index * block_rows, block_rows, 1)
        target = jnp.where(block_tags[0] == self_owner, block_tags[1], frame_count)
        return total + jnp.dot(
            block_values, slot_table(target, frame_count), preferred_element_type=jnp.float32
        )

    gathered_sum = lax.fori_loop(
        0, piece_rows // block_rows, add_block, jnp.zeros((mel_bins, frame_count), jnp.float32)
    )
    holder_mel = gathered_sum.astype(jnp.bfloat16)
    utterance_frames_length = holder_utterance_length[self_owner]
    wave = vocoder_synthesize(
        holder_mel,
        utterance_frames_length,
        input_conv_weight,
        input_conv_bias,
        transposed_conv_weight,
        transposed_conv_bias,
        snake_freq_first,
        dilated_conv_weight,
        dilated_conv_bias,
        snake_freq_second,
        second_conv_weight,
        second_conv_bias,
    )
    return wave[None]


def solution(mesh):
    return jax.shard_map(
        local,
        mesh=mesh,
        in_specs=(
            P("branch", "seq", None),
            P(None, "seq"),
            P(),
            P(),
            P(),
            P(),
            P(),
            P(),
            P(),
            P(),
            P(),
            P(),
            P(),
            P(),
            P(),
            P(),
            P(),
            P(),
            P(),
            P("seq"),
            P("seq"),
            P(),
        ),
        out_specs=P(("branch", "seq"), None, None),
        check_vma=False,
    )
```

profile of v0, /device:TPU:0, one launch (start us, length us, event | category | flops | bytes accessed | tf_op | source)
XLA Modules:
  0.0 257.8 jit_solution(13189924340032700017)
XLA Ops:
  6.6 1.0 slice_add_fusion
  7.6 1.7 convert_reduce_fusion
  9.3 2.0 fusion.61
  11.3 12.4 %fusion.91 = (f32[768]{0:T(1024)S(1)}, f32[768,1024]{1,0:T(8,128)}) fusion(f32[1024]{0:T(1024)S(1)} %copy-done.16, bf16[2048,1024]{1,0:T(8,128)(2,1)} %param.29, bf16[1024,2048]{1,0:T(8,128)(2,1)} %param.27, f32[2048]{0:T(1024)S(1)} %copy-done.15, bf16[1,768,1024]{2,1,0:T(8,128)(2,1)S(1)} %copy-done.5, f32[1024]{0:T(1024)S(1)} %bitcast.100, ...), kind=kOutput, calls=%fused_computation.105 | convolution fusion | flops 6466829312 | bytes 13140992 | tf_op jit(solution)/shard_map/dot_general | solution.py:53
  23.7 2.5 multiply_reduce_fusion
  26.5 0.8 fusion.73
  27.9 1.2 collective-permute-done
  31.3 71.1 %all_gather.7 = s32[2,12288]{1,0:T(2,128)S(1)} all-gather(s32[2,384]{1,0:T(2,128)S(1)} %pad_add_fusion), channel_id=1, replica_groups=mesh['branch'=2,'seq'=16] {'branch','seq'}, dimensions={1}, use_global_device_ids=true | all-gather | bytes 101376 | tf_op jit(solution)/shard_map/all_gather | solution.py:201
  103.0 36.7 %while.14 = (s32[]{:T(128)}, f32[100,768]{1,0:T(8,128)S(1)}, bf16[100,12288]{1,0:T(8,128)(2,1)}, s32[2,12288]{1,0:T(2,128)S(1)}, s32[]{:T(128)}, /*index=5*/s32[]{:T(128)}, s32[]{:T(128)}, s32[]{}, s32[]{:T(128)}, s32[]{:T(128)}) while((s32[]{:T(128)}, f32[100,768]{1,0:T(8,128)S(1)}, bf16[100,12288]{1,0:T(8,128)(2,1)}, ...), condition=%wide.region_5.6_spmd.clone, body=%wide.region_4.5_spmd.clone.sunk | while | flops 79191048 | bytes 729273 | solution.py:213
  103.1 1.4 fusion.105
  104.7 1.4 fusion.105
  106.2 1.4 fusion.105
  107.7 1.4 fusion.105
  109.3 1.4 fusion.105
  110.8 1.4 fusion.105
  112.3 1.4 fusion.105
  113.9 1.4 fusion.105
  115.4 1.4 fusion.105
  116.9 1.4 fusion.105
  118.5 1.4 fusion.105
  120.0 1.4 fusion.105
  121.5 1.4 fusion.105
  123.0 1.4 fusion.105
  124.6 1.4 fusion.105
  126.1 1.4 fusion.105
  127.6 1.4 fusion.105
  129.2 1.4 fusion.105
  130.7 1.4 fusion.105
  132.2 1.4 fusion.105
  133.8 1.4 fusion.105
  135.3 1.4 fusion.105
  136.8 1.4 fusion.105
  138.4 1.4 fusion.105
  140.2 1.1 concatenate.12
  141.3 9.2 %convolution_bitcast_fusion = f32[4096,768]{0,1:T(8,128)} fusion(bf16[4096,512]{1,0:T(8,128)(2,1)} %param.35, bf16[700,768]{1,0:T(8,128)(2,1)S(1)} %concatenate.12, bf16[700,512]{1,0:T(8,128)(2,1)S(1)} %copy-done, f32[512]{0:T(512)S(1)} %copy-done.17, pred[768]{0:T(1024)(128)(4,1)S(1)} %iota_compare_fusion.5), kind=kOutput, calls=%fused_computation.25 | convolution fusion | flops 3772907520 | bytes 18572032 | tf_op jit(solution)/shard_map/dot_general | solution.py:118
  150.5 7.3 %fusion.90 = (f32[1024,768]{0,1:T(8,128)}, f32[1024,768]{0,1:T(8,128)}) fusion(f32[4096,768]{0,1:T(8,128)} %convolution_bitcast_fusion), kind=kLoop, calls=%fused_computation.104 | loop fusion | bytes 12582912 | tf_op jit(solution)/shard_map/slice | solution.py:123
  157.8 1.4 copy-done.2
  159.2 3.1 %slice.108 = f32[2048,768]{0,1:T(8,128)} slice(f32[4096,768]{0,1:T(8,128)S(1)} %copy-done.2), slice={[1024:3072], [0:768]} | slice | bytes 12582912 | tf_op jit(solution)/shard_map/slice | solution.py:122
  162.3 5.2 %slice.100 = f32[4,256,768]{1,0,2:T(4,128)} reshape(f32[1024,768]{0,1:T(8,128)} %get-tuple-element.131) | data formatting | bytes 6291456 | tf_op jit(solution)/shard_map/slice | solution.py:124
  167.5 5.2 %slice.97 = f32[4,256,768]{1,0,2:T(4,128)} reshape(f32[1024,768]{0,1:T(8,128)} %get-tuple-element.130) | data formatting | bytes 6291456 | tf_op jit(solution)/shard_map/slice | solution.py:123
  172.7 6.0 %copy.24 = f32[96,8,8,256]{3,2,1,0:T(8,128)S(1)} copy(f32[96,8,8,256]{3,1,2,0:T(8,128)} %bitcast.95) | data formatting | bytes 12582912
  178.8 1.1 pad_slice_fusion
  179.9 27.0 %fusion.54 = (bf16[256,6144]{0,1:T(8,128)(2,1)S(1)}, bf16[256,6144]{0,1:T(8,128)(2,1)S(1)}) fusion(f32[256]{0:T(256)S(1)} %copy-done.8, f32[256]{0:T(256)S(1)} %copy-done.9, f32[4,256,768]{1,0,2:T(4,128)S(1)} %get-tuple-element.149, f32[4,256,768]{1,0,2:T(4,128)S(1)} %get-tuple-element.150, f32[96,8,8,256]{3,2,1,0:T(8,128)S(1)} %copy.24, ...), kind=kLoop, calls=%fused_computation.43 | loop fusion | flops 17301504 | bytes 18882560 | tf_op jit(solution)/shard_map/convert_element_type | solution.py:132
  206.9 1.7 pad_slice_fusion.5
  208.7 29.9 %add_convert_fusion = bf16[256,6144]{0,1:T(8,128)(2,1)S(1)} fusion(f32[256]{0:T(256)S(1)} %copy-done.18, f32[256]{0:T(256)S(1)} %copy-done.19, bf16[768,256]{1,0:T(8,128)(2,1)S(1)} %copy-done.12, bf16[256,6144]{0,1:T(8,128)(2,1)S(1)} %get-tuple-element.135, bf16[256,6144]{0,1:T(8,128)(2,1)S(1)} %get-tuple-element.128, ...), kind=kOutput, calls=%fused_computation.48 | convolution fusion | flops 2455240704 | bytes 12984320 | tf_op jit(solution)/shard_map/dot_general | solution.py:86
  238.5 1.7 pad_slice_fusion.3
  240.2 6.0 %fusion.40 = bf16[1,256,6144]{1,2,0:T(8,128)(2,1)} fusion(bf16[768,256]{1,0:T(8,128)(2,1)S(1)} %copy-done.13, bf16[256,6144]{0,1:T(8,128)(2,1)S(1)} %get-tuple-element.133, bf16[256,6144]{0,1:T(8,128)(2,1)S(1)} %add_convert_fusion, bf16[256,6144]{0,1:T(8,128)(2,1)S(1)} %get-tuple-element.132, bf16[256,6144]{0,1:T(8,128)(2,1)S(1)} %get-tuple-element.129, ...), kind=kOutput, calls=%fused_computation.31 | convolution fusion | flops 2452094976 | bytes 16129024 | tf_op jit(solution)/shard_map/dot_general | solution.py:86
  246.3 4.6 %copy.23 = bf16[1,256,6144]{2,1,0:T(8,128)(2,1)} copy(bf16[1,256,6144]{1,2,0:T(8,128)(2,1)} %fusion.40) | data formatting | bytes 6291456 | tf_op jit(solution)/shard_map/broadcast_in_dim | solution.py:232
  (89 shorter events, 5.4 us)
Async XLA Ops:
  6.5 134.7 %copy-start = (bf16[700,512]{1,0:T(8,128)(2,1)S(1)}, bf16[700,512]{1,0:T(8,128)(2,1)}, u32[]{:S(2)}) copy-start(bf16[700,512]{1,0:T(8,128)(2,1)} %param.33) | copy-start | bytes 2150404
  6.5 4.7 %copy-start.5 = (bf16[1,768,1024]{2,1,0:T(8,128)(2,1)S(1)}, bf16[1,768,1024]{2,1,0:T(8,128)(2,1)}, u32[]{:S(2)}) copy-start(bf16[1,768,1024]{2,1,0:T(8,128)(2,1)} %param.24) | copy-start | bytes 4718596
  6.5 4.7 %copy-start.15 = (f32[2048]{0:T(1024)S(1)}, f32[2048]{0:T(1024)}, u32[]{:S(2)}) copy-start(f32[2048]{0:T(1024)} %param.28) | copy-start | bytes 24580
  6.5 4.7 %copy-start.16 = (f32[1024]{0:T(1024)S(1)}, f32[1024]{0:T(1024)}, u32[]{:S(2)}) copy-start(f32[1024]{0:T(1024)} %param.30) | copy-start | bytes 12292
  6.5 96.5 %all-gather.2.cloned.1.call-start = ((), (), s32[]{:S(2)}) async-start(), calls=%async_computation | async-start | bytes 2635776 | tf_op jit(solution)/shard_map/all_gather | solution.py:200
  11.3 15.0 %copy-start.14 = (bf16[1024,100]{0,1:T(8,128)(2,1)S(1)}, bf16[1024,100]{0,1:T(8,128)(2,1)}, u32[]{:S(2)}) copy-start(bf16[1024,100]{0,1:T(8,128)(2,1)} %param.31) | copy-start | bytes 614404
  23.7 2.8 %copy-start.6 = (f32[768,1024]{1,0:T(8,128)S(1)}, f32[768,1024]{1,0:T(8,128)}, u32[]{:S(2)}) copy-start(f32[768,1024]{1,0:T(8,128)} %get-tuple-element.148) | copy-start | bytes 9437188
  23.7 2.8 %copy-start.21 = (f32[100]{0:T(128)S(1)}, f32[100]{0:T(128)}, u32[]{:S(2)}) copy-start(f32[100]{0:T(128)} %param.32) | copy-start | bytes 1204
  23.7 5.4 %copy-start.7 = (f32[100,768]{1,0:T(8,128)S(1)}, f32[100,768]{1,0:T(8,128)}, u32[]{:S(2)}) copy-start(f32[100,768]{1,0:T(8,128)} %param.25) | copy-start | bytes 921604
  26.2 3.7 %copy-start.10 = (s32[768]{0:T(1024)S(1)}, s32[768]{0:T(1024)}, u32[]{:S(2)}) copy-start(s32[768]{0:T(1024)} %param.44) | copy-start | bytes 9220
  26.2 3.7 %copy-start.11 = (s32[768]{0:T(1024)S(1)}, s32[768]{0:T(1024)}, u32[]{:S(2)}) copy-start(s32[768]{0:T(1024)} %param.43) | copy-start | bytes 9220
  26.2 3.8 %copy-start.22 = (s32[32]{0:T(128)S(1)}, s32[32]{0:T(128)}, u32[]{:S(2)}) copy-start(s32[32]{0:T(128)} %param.45) | copy-start | bytes 388
  27.4 1.8 collective-permute-start
  103.0 38.2 %copy-start.17 = (f32[512]{0:T(512)S(1)}, f32[512]{0:T(512)}, u32[]{:S(2)}) copy-start(f32[512]{0:T(512)} %param.34) | copy-start | bytes 6148
  150.5 8.7 %copy-start.2 = (f32[4096,768]{0,1:T(8,128)S(1)}, f32[4096,768]{0,1:T(8,128)}, u32[]{:S(2)}) copy-start(f32[4096,768]{0,1:T(8,128)} %convolution_bitcast_fusion) | copy-start | bytes 37748740
  172.7 6.0 %copy-start.3 = (f32[4,256,768]{1,0,2:T(4,128)S(1)}, f32[4,256,768]{1,0,2:T(4,128)}, u32[]{:S(2)}) copy-start(f32[4,256,768]{1,0,2:T(4,128)} %slice.100) | copy-start | bytes 9437188
  172.7 6.0 %copy-start.4 = (f32[4,256,768]{1,0,2:T(4,128)S(1)}, f32[4,256,768]{1,0,2:T(4,128)}, u32[]{:S(2)}) copy-start(f32[4,256,768]{1,0,2:T(4,128)} %slice.97) | copy-start | bytes 9437188
  178.7 1.2 copy-start.8
  178.8 1.2 copy-start.9
  206.9 1.7 copy-start.12
  206.9 1.7 copy-start.18
  206.9 1.7 copy-start.19
  238.5 1.7 copy-start.13
  238.5 1.7 copy-start.20
  240.2 10.7 %copy-start.1 = (bf16[700,512]{1,0:T(8,128)(2,1)S(1)}, bf16[700,512]{1,0:T(8,128)(2,1)}, u32[]{:S(2)}) copy-start(bf16[700,512]{1,0:T(8,128)(2,1)} %param.33) | copy-start | bytes 2150404
Sparse Core Ops, SparseCore 0:
  30.0 58.6 all-gather.1
where the time goes:
time: 259 us; the launch traced here: 258 us
  matrix products  92.4 us (36%)
  blocking collectives  71.1 us (27%)
  local copies, waits for them, and re-layouts  39.9 us (15%)
  other arithmetic  37.5 us (14%)
  between operations  14.4 us (6%)
    all_gather x1, blocking collectives, local(): tag_rows = lax.all_gather(frame_tags, ('branch', 'seq'), axis=1, tiled=True)  71.1 us
    dot_general x2, matrix products, dilated_output(): lax.dot_general(weight, stacked, (((0,), (0,)), ((), ())), preferred_elem...  35.9 us
    dot_general x24, matrix products, add_block(): jnp.dot(block_values, slot_table(target, frame_count), preferred_element_...  34.1 us
    convert_element_type x1, other arithmetic, vocoder_synthesize(): snake(upsampled.astype(jnp.float32), snake_freq_first).astype(jnp.bfloat16)  27 us
    slice x2, local copies, waits for them, and re-layouts, vocoder_synthesize(): early_part = shifted(phases[UP + pad_up:], -1)  12.5 us
    dot_general x1, matrix products, velocity(): jnp.dot(active, feedforward_out_weight, preferred_element_type=jnp.float32)  12.4 us
    dot_general x1, matrix products, vocoder_synthesize(): jnp.dot(transposed_conv_weight, pre_out, preferred_element_type=jnp.float32)  9.24 us
    unnamed x47, local copies, waits for them, and re-layouts  7.81 us
  transfers between devices with their start and end apart: 2, of which 1 were waited for; matrix products, arithmetic and copies ran while one was open for 1% of the time, Pallas kernels for 0%

commit v1 on v0

v1 whole, which is shorter than its diff:
```python
import math

import jax
import jax.numpy as jnp
from jax import lax
from jax.experimental import pallas as pl
from jax.experimental.pallas import tpu as pltpu
from jax.sharding import PartitionSpec as P

UP = 8
KT = 16
KPRE = 7
DILATION_RATE = 3
NFE = 16

GUIDE = 2.0
LANES = 128
PAD = 16
CHUNK = 256
GROUP = 32
SERIES = tuple(
    factor * math.pi ** (2 * power + 2)
    for power, factor in enumerate(
        (
            0.9999998490771234,
            -0.3333321377542852,
            0.04444128701478595,
            -0.0031707593706167504,
            0.00013871416537404423,
            -3.540445572482011e-06,
        )
    )
)


def partner(block, axis, distance):
    count = lax.axis_size(axis)
    route = []
    for low in range(count):
        high = low | 1 << distance
        if high != low and high < count:
            route += [(low, high), (high, low)]
    return lax.ppermute(block, axis, route)


def layer_norm(row_block):
    row_mean = jnp.mean(row_block, axis=-1, keepdims=True)
    centred = row_block - row_mean
    row_var = jnp.mean(centred * centred, axis=-1, keepdims=True)
    return centred * lax.rsqrt(row_var + 1e-06)


def velocity(
    row_block,
    modulation,
    feedforward_in_weight,
    feedforward_in_bias,
    feedforward_out_weight,
    feedforward_out_bias,
    mel_velocity_weight,
    mel_velocity_bias,
):
    residual_in = row_block.astype(jnp.float32)
    normed = (layer_norm(residual_in) * (1.0 + modulation[1]) + modulation[0]).astype(jnp.bfloat16)
    inner_pre = (
        jnp.dot(normed, feedforward_in_weight, preferred_element_type=jnp.float32)
        + feedforward_in_bias
    )
    active = jax.nn.gelu(inner_pre, approximate=True).astype(jnp.bfloat16)
    back_proj = (
        jnp.dot(active, feedforward_out_weight, preferred_element_type=jnp.float32)
        + feedforward_out_bias
    )
    block_out = residual_in + modulation[2] * back_proj
    final_norm = (layer_norm(block_out) * (1.0 + modulation[4]) + modulation[3]).astype(
        jnp.bfloat16
    )
    speed = jnp.dot(final_norm, mel_velocity_weight, preferred_element_type=jnp.float32)
    return speed + mel_velocity_bias


def snake(signal, turns, inverse):
    spin = signal * turns
    spin = spin - jnp.round(spin)
    square = spin * spin
    series = SERIES[-1]
    for factor in SERIES[-2::-1]:
        series = series * square + factor
    return signal + (series * square) * inverse


def product(left, right, left_dim, right_dim):
    return lax.dot_general(
        left, right, (((left_dim,), (right_dim,)), ((), ())), preferred_element_type=jnp.float32
    )


def vocoder_kernel(
    length_ref,
    mel_ref,
    pre_w_ref,
    pre_b_ref,
    up_w_ref,
    up_b_ref,
    turns_first_ref,
    inverse_first_ref,
    dil_w_ref,
    dil_b_ref,
    turns_second_ref,
    inverse_second_ref,
    second_w_ref,
    second_b_ref,
    weave_ref,
    out_ref,
    mel_pad,
    pre_pad,
    up_keep,
    act_first,
    act_second,
):
    rows = mel_ref.shape[0]
    channels = out_ref.shape[0]
    chunk = math.gcd(rows, CHUNK)
    length = length_ref[0]
    lanes = mel_ref.shape[1]
    bf16 = jnp.bfloat16

    mel_pad[pl.ds(0, PAD)] = jnp.zeros((PAD, lanes), jnp.float32)
    mel_pad[pl.ds(PAD + rows, PAD)] = jnp.zeros((PAD, lanes), jnp.float32)
    skip = length_ref[1]
    rolled = pltpu.roll(mel_ref[...].astype(jnp.float32), lax.rem(rows - skip, rows), 0)
    inside = lax.broadcasted_iota(jnp.int32, (rows, 1), 0) < length
    mel_pad[pl.ds(PAD, rows)] = jnp.where(inside, rolled, 0.0)
    edge = jnp.zeros((PAD, pre_pad.shape[1]), bf16)
    pre_pad[pl.ds(0, PAD)] = edge
    pre_pad[pl.ds(PAD + rows, PAD)] = edge
    edge = jnp.zeros((UP, PAD, channels), bf16)
    for act in (act_first, act_second):
        act[:, pl.ds(0, PAD)] = edge
        act[:, pl.ds(PAD + rows, PAD)] = edge

    def keep_of(start):
        return start + lax.broadcasted_iota(jnp.int32, (chunk, 1), 0) < length

    def moved(window, offset):
        size = window.shape[0]
        wide = window.astype(jnp.float32)
        return pltpu.roll(wide, size - PAD - offset, 0)[:chunk]

    @pl.loop(0, rows // chunk)
    def _(step):
        start = pl.multiple_of(step * chunk, chunk)
        window = mel_pad[pl.ds(start, chunk + 2 * PAD)]
        stacked = jnp.concatenate(
            [moved(window, k - KPRE // 2).astype(bf16) for k in range(KPRE)], axis=1
        )
        pre = product(stacked, pre_w_ref[...], 1, 0) + pre_b_ref[...]
        pre = jnp.where(keep_of(start), pre, 0.0).astype(bf16)
        pre_pad[pl.ds(PAD + start, chunk)] = pre

    half = UP // 2

    @pl.loop(0, rows // chunk)
    def _(step):
        start = pl.multiple_of(step * chunk, chunk)
        keep = keep_of(start)
        window = pre_pad[pl.ds(start, chunk + 2 * PAD)]
        here = window[PAD : PAD + chunk]
        before = moved(window, -1).astype(bf16)
        after = moved(window, 1).astype(bf16)
        for phase in range(UP):
            tap = phase + half
            other = tap + UP if phase < half else tap - UP
            side = before if phase < half else after
            value = product(here, up_w_ref[pl.ds(tap * channels, channels)], 1, 1)
            value = value + product(side, up_w_ref[pl.ds(other * channels, channels)], 1, 1)
            value = jnp.where(keep, value + up_b_ref[...], 0.0).astype(bf16)
            up_keep[phase, pl.ds(start, chunk)] = value
            first = snake(value.astype(jnp.float32), turns_first_ref[...], inverse_first_ref[...])
            act_first[phase, pl.ds(PAD + start, chunk)] = first.astype(bf16)

    def tap_of(act, start, phase):
        frame, inner = phase // UP, phase % UP
        if frame == 0:
            return act[inner, pl.ds(PAD + start, chunk)]
        return moved(act[inner, pl.ds(start, chunk + 2 * PAD)], frame).astype(bf16)

    def conv_of(act, start, phase, spacing, weight_ref):
        stacked = jnp.concatenate(
            [tap_of(act, start, phase + k * spacing) for k in (-1, 0, 1)], axis=1
        )
        return product(stacked, weight_ref[...], 1, 0)

    @pl.loop(0, rows // chunk)
    def _(step):
        start = pl.multiple_of(step * chunk, chunk)
        keep = keep_of(start)
        for phase in range(UP):
            inner = conv_of(act_first, start, phase, DILATION_RATE, dil_w_ref)
            inner = jnp.where(keep, inner + dil_b_ref[...], 0.0)
            second = snake(inner, turns_second_ref[...], inverse_second_ref[...])
            act_second[phase, pl.ds(PAD + start, chunk)] = second.astype(bf16)

    @pl.loop(0, rows // chunk)
    def _(step):
        start = pl.multiple_of(step * chunk, chunk)
        keep = keep_of(start)
        waves = []
        for phase in range(UP):
            outer = conv_of(act_second, start, phase, 1, second_w_ref)
            outer = jnp.where(keep, outer + second_b_ref[...], 0.0)
            kept = up_keep[phase, pl.ds(start, chunk)].astype(jnp.float32)
            waves.append((kept + outer).astype(bf16))
        for group in range(chunk // GROUP):
            picked = jnp.concatenate(
                [wave[group * GROUP : (group + 1) * GROUP] for wave in waves], axis=0
            )
            woven = product(picked, weave_ref[...], 0, 0).astype(bf16)
            width = UP * GROUP
            column = pl.multiple_of(start * UP + group * width, width)
            out_ref[:, pl.ds(column, width)] = woven


def vocoder_synthesize(
    holder_mel,
    utterance_frames_length,
    input_conv_weight,
    input_conv_bias,
    transposed_conv_weight,
    transposed_conv_bias,
    snake_freq_first,
    dilated_conv_weight,
    dilated_conv_bias,
    snake_freq_second,
    second_conv_weight,
    second_conv_bias,
):
    rows, lanes = holder_mel.shape
    channels = transposed_conv_weight.shape[0] // KT
    hidden_channels = input_conv_weight.shape[1]
    bins = input_conv_weight.shape[0] // KPRE
    pre_weight = input_conv_weight.reshape(KPRE, bins, hidden_channels)
    pre_weight = jnp.pad(pre_weight, ((0, 0), (0, lanes - bins), (0, 0)))
    pre_weight = pre_weight.reshape(KPRE * lanes, hidden_channels)
    width = UP * GROUP
    source = jnp.arange(width)[:, None]
    weave = (source % GROUP) * UP + source // GROUP == jnp.arange(width)[None, :]
    vmem = pl.BlockSpec(memory_space=pltpu.VMEM)
    return pl.pallas_call(
        vocoder_kernel,
        out_shape=jax.ShapeDtypeStruct((channels, rows * UP), jnp.bfloat16),
        in_specs=[pl.BlockSpec(memory_space=pltpu.SMEM)] + [vmem] * 14,
        out_specs=vmem,
        scratch_shapes=[
            pltpu.VMEM((rows + 2 * PAD, lanes), jnp.float32),
            pltpu.VMEM((rows + 2 * PAD, hidden_channels), jnp.bfloat16),
            pltpu.VMEM((UP, rows, channels), jnp.bfloat16),
            pltpu.VMEM((UP, rows + 2 * PAD, channels), jnp.bfloat16),
            pltpu.VMEM((UP, rows + 2 * PAD, channels), jnp.bfloat16),
        ],
        compiler_params=pltpu.CompilerParams(vmem_limit_bytes=40 * 1024 * 1024),
        cost_estimate=pl.CostEstimate(
            flops=2 * rows * (700 * 512 + 16 * 256 * 512 + 48 * 256 * 256),
            bytes_accessed=10_000_000,
            transcendentals=0,
        ),
        name="vocoder",
    )(
        utterance_frames_length,
        holder_mel,
        pre_weight,
        input_conv_bias[None],
        transposed_conv_weight,
        transposed_conv_bias[None],
        (snake_freq_first / math.pi)[None],
        (1.0 / snake_freq_first)[None],
        dilated_conv_weight,
        dilated_conv_bias[None],
        (snake_freq_second / math.pi)[None],
        (1.0 / snake_freq_second)[None],
        second_conv_weight,
        second_conv_bias[None],
        weave.astype(jnp.bfloat16),
    )


def begins(frame_holder, frame_position, holder_utterance_length):
    frame_count = frame_holder.shape[0]
    owners = jnp.arange(holder_utterance_length.shape[0], dtype=jnp.int32)
    frame = lax.axis_index("seq") * frame_count + jnp.arange(frame_count, dtype=jnp.int32)
    opens = (frame_holder[:, None] == owners[None, :]) & (frame_position == 0)[:, None]
    found = jnp.sum(jnp.where(opens, frame[:, None], 0), axis=0)
    return lax.psum(found.astype(jnp.float32), "seq").astype(jnp.int32)


def local(
    hidden,
    noisy_mel_state,
    modulation,
    feedforward_in_weight,
    feedforward_in_bias,
    feedforward_out_weight,
    feedforward_out_bias,
    mel_velocity_weight,
    mel_velocity_bias,
    input_conv_weight,
    input_conv_bias,
    transposed_conv_weight,
    transposed_conv_bias,
    snake_freq_first,
    dilated_conv_weight,
    dilated_conv_bias,
    snake_freq_second,
    second_conv_weight,
    second_conv_bias,
    frame_holder,
    frame_position,
    holder_utterance_length,
):
    step_size = math.cos(0.5 * math.pi * (NFE - 1) / NFE)
    own_velocity = velocity(
        hidden[0],
        modulation,
        feedforward_in_weight,
        feedforward_in_bias,
        feedforward_out_weight,
        feedforward_out_bias,
        mel_velocity_weight,
        mel_velocity_bias,
    )
    frame_count, mel_bins = own_velocity.shape
    half_rows = frame_count // 2
    branch_side = lax.axis_index("branch")
    own_half = lax.dynamic_slice_in_dim(own_velocity, branch_side * half_rows, half_rows, 0)
    other_half = lax.dynamic_slice_in_dim(own_velocity, (1 - branch_side) * half_rows, half_rows, 0)
    peer_half = partner(other_half, "branch", 0)
    conditional = jnp.where(branch_side == 0, own_half, peer_half)
    unconditional = jnp.where(branch_side == 0, peer_half, own_half)
    guided = (1.0 + GUIDE) * conditional - GUIDE * unconditional
    noisy_half = lax.dynamic_slice_in_dim(noisy_mel_state, branch_side * half_rows, half_rows, 1)
    refined = (noisy_half.T + step_size * guided).astype(jnp.bfloat16)
    refined = jnp.pad(refined, ((0, 0), (0, -mel_bins % LANES)))

    self_owner = lax.axis_index(("branch", "seq"))
    utterance_frames_length = holder_utterance_length[self_owner]
    begin = begins(frame_holder, frame_position, holder_utterance_length)[self_owner]
    frames = lax.all_gather(refined, ("seq", "branch"), axis=0, tiled=True)
    first = jnp.minimum(begin, frames.shape[0] - frame_count)
    holder_mel = lax.dynamic_slice_in_dim(frames, first, frame_count, 0)
    utterance_frames_length = jnp.stack([utterance_frames_length, begin - first])
    wave = vocoder_synthesize(
        holder_mel,
        utterance_frames_length,
        input_conv_weight,
        input_conv_bias,
        transposed_conv_weight,
        transposed_conv_bias,
        snake_freq_first,
        dilated_conv_weight,
        dilated_conv_bias,
        snake_freq_second,
        second_conv_weight,
        second_conv_bias,
    )
    return wave[None]


def solution(mesh):
    return jax.shard_map(
        local,
        mesh=mesh,
        in_specs=(
            P("branch", "seq", None),
            P(None, "seq"),
            P(),
            P(),
            P(),
            P(),
            P(),
            P(),
            P(),
            P(),
            P(),
            P(),
            P(),
            P(),
            P(),
            P(),
            P(),
            P(),
            P(),
            P("seq"),
            P("seq"),
            P(),
        ),
        out_specs=P(("branch", "seq"), None, None),
        check_vma=False,
    )
```

time: 259 us -> 125 us (0.48)
  matrix products: 92.4 us -> 15.2 us
  local copies, waits for them, and re-layouts: 39.9 us -> 5.44 us
  other arithmetic: 37.5 us -> 7.98 us
  blocking collectives: 71.1 us -> 43.6 us
  Pallas kernels: 0 us -> 21.8 us
  waiting for transfers between devices: 1.28 us -> 15.6 us
    dot_general x28 -> x1, matrix products: 80 us -> 2.73 us  [velocity(): jnp.dot(final_norm, mel_velocity_weight, preferred_element_type=jnp.float32)]
    all_gather x1 -> x0, blocking collectives: 71.1 us -> none  [local(): tag_rows = lax.all_gather(frame_tags, ('branch', 'seq'), axis=1, tiled=True)]
    psum x0 -> x1, blocking collectives: none -> 43.6 us  [begins(): return lax.psum(found.astype(jnp.float32), 'seq').astype(jnp.int32)]
    convert_element_type x3 -> x4, other arithmetic: 27.7 us -> 0.17 us  [the longest x1 0.1 us: vocoder_synthesize(): weave.astype(jnp.bfloat16)]
    slice x8 -> x0, local copies, waits for them, and re-layouts: 25.6 us -> none  [the longest x2 12.5 us: vocoder_synthesize(): early_part = shifted(phases[UP + pad_up:], -1)]
    pallas_call x0 -> x1, Pallas kernels: none -> 21.8 us  [vocoder_synthesize(): pl.pallas_call(vocoder_kernel, out_shape=jax.ShapeDtypeStruct((channels,...]
    all_gather x1, waiting for transfers between devices: 0.02 us -> 14.6 us  [local(): frames = lax.all_gather(refined, ('seq', 'branch'), axis=0, tiled=True)]
    unnamed x47 -> x39, local copies, waits for them, and re-layouts: 7.81 us -> 2.41 us
  transfers between devices with their start and end apart: 2 -> 2, of which waited for: 1 -> 2; matrix products, arithmetic and copies ran while one was open for 1% -> 2% of each run, Pallas kernels for 0% -> 0%
where the time goes in v1:
time: 125 us
  blocking collectives  43.6 us (35%)
  Pallas kernels  21.8 us (17%)
  waiting for transfers between devices  15.6 us (12%)
  matrix products  15.2 us (12%)
  between operations  14.9 us (12%)
  other arithmetic  7.98 us (6%)
  local copies, waits for them, and re-layouts  5.44 us (4%)
    psum x1, blocking collectives, begins(): return lax.psum(found.astype(jnp.float32), 'seq').astype(jnp.int32)  43.6 us
    pallas_call x1, Pallas kernels, vocoder_synthesize(): pl.pallas_call(vocoder_kernel, out_shape=jax.ShapeDtypeStruct((channels,...  21.8 us
    all_gather x1, waiting for transfers between devices, local(): frames = lax.all_gather(refined, ('seq', 'branch'), axis=0, tiled=True)  14.6 us
    dot_general x1, matrix products, velocity(): jnp.dot(active, feedforward_out_weight, preferred_element_type=jnp.float32)  12.4 us
    reduce_sum x2, other arithmetic, layer_norm(): row_var = jnp.mean(centred * centred, axis=-1, keepdims=True)  4.34 us
    dot_general x1, matrix products, velocity(): jnp.dot(final_norm, mel_velocity_weight, preferred_element_type=jnp.float32)  2.73 us
  transfers between devices with their start and end apart: 2, of which 2 were waited for; matrix products, arithmetic and copies ran while one was open for 2% of the time, Pallas kernels for 0%

profile of v1, /device:TPU:0, one launch (start us, length us, event | category | flops | bytes accessed | tf_op | source)
XLA Modules:
  0.0 125.1 jit_solution(15045418343941491371)
XLA Ops:
  6.5 0.0 copy-start
  6.5 0.0 all-gather.2.cloned.1.call-start
  6.6 1.0 slice_add_fusion
  7.6 1.7 %convert_reduce_fusion = f32[768]{0:T(1024)S(1)} fusion(bf16[1,768,1024]{2,1,0:T(8,128)(2,1)} %param.22), kind=kLoop, calls=%fused_computation.9 | loop fusion | flops 1572096 | bytes 1575936 | tf_op jit(solution)/shard_map/reduce_sum | solution.py:47
  9.3 2.0 %fusion.12 = f32[768]{0:T(1024)S(1)} fusion(bf16[1,768,1024]{2,1,0:T(8,128)(2,1)} %param.22, f32[768]{0:T(1024)S(1)} %broadcast_multiply_fusion.1), kind=kLoop, calls=%fused_computation.15 | loop fusion | flops 3144960 | bytes 1579008 | tf_op jit(solution)/shard_map/reduce_sum | solution.py:49
  11.2 0.0 copy-done.8
  11.2 0.0 copy-done.15
  11.3 0.0 copy-done.16
  11.3 12.4 %fusion.36 = (f32[768]{0:T(1024)S(1)}, f32[768,1024]{1,0:T(8,128)}) fusion(f32[1024]{0:T(1024)S(1)} %copy-done.16, bf16[2048,1024]{1,0:T(8,128)(2,1)} %param.27, bf16[1024,2048]{1,0:T(8,128)(2,1)} %param.25, f32[2048]{0:T(1024)S(1)} %copy-done.15, bf16[1,768,1024]{2,1,0:T(8,128)(2,1)S(1)} %copy-done.8, f32[1024]{0:T(1024)S(1)} %bitcast.58, ...), kind=kOutput, calls=%fused_computation.63 | convolution fusion | flops 6466829312 | bytes 13140992 | tf_op jit(solution)/shard_map/dot_general | solution.py:71
  23.7 2.4 %multiply_reduce_fusion = f32[768]{0:T(1024)S(1)} fusion(f32[768,1024]{1,0:T(8,128)} %get-tuple-element.15, f32[768]{0:T(1024)S(1)} %broadcast_multiply_fusion), kind=kLoop, calls=%fused_computation.20 | loop fusion | flops 2358528 | bytes 3151872 | tf_op jit(solution)/shard_map/reduce_sum | solution.py:49
  26.1 0.0 copy-done.14
  26.1 0.0 copy-done.17
  26.1 0.0 copy-start.10
  26.1 0.0 copy-start.11
  26.2 0.0 copy-start.18
  26.2 0.0 copy-start.9
  26.2 2.7 %fusion.22 = f32[768,100]{1,0:T(8,128)S(1)} fusion(bf16[1024,100]{0,1:T(8,128)(2,1)S(1)} %copy-done.14, f32[768,1024]{1,0:T(8,128)} %get-tuple-element.15, f32[1024]{0:T(1024)S(1)} %bitcast.57, f32[1024]{0:T(1024)S(1)} %bitcast.56, f32[768]{0:T(1024)S(1)} %add_rsqrt_fusion, f32[768]{0:T(1024)S(1)} %broadcast_multiply_fusion, f32[100]{0:T(128)S(1)} %copy-done.17), kind=kOutput, calls=%fused_computation.26 | convolution fusion | flops 161295360 | bytes 3672464 | tf_op jit(solution)/shard_map/dot_general | solution.py:78
  28.9 0.0 copy-start.12
  28.9 0.0 copy-start.13
  28.9 0.0 copy-start.2
  29.0 0.0 copy-start.3
  29.0 0.0 copy-start.4
  29.0 0.0 copy-start.5
  29.0 0.0 copy-start.6
  29.0 0.0 copy-start.7
  29.0 0.5 collective-permute-start
  29.6 0.0 copy-done
  29.6 0.1 copy.28
  29.7 0.9 collective-permute-done
  30.6 0.1 fusion.26
  30.7 0.7 pad.8
  31.4 0.0 all-gather.2.cloned.1.call-update
  31.4 0.0 copy-done.10
  31.4 0.0 copy-done.11
  31.4 0.1 select_reduce_fusion
  31.6 43.6 %psum.7 = f32[32]{0:T(128)S(1)} all-reduce(f32[32]{0:T(128)S(1)} %convert_element_type.31), channel_id=1, replica_groups=mesh['branch'=2,'seq'=16] {'seq'}, use_global_device_ids=true, to_apply=%region_1.0 | all-reduce | flops 32 | bytes 256 | tf_op jit(solution)/shard_map/psum | solution.py:293
  75.2 0.6 dynamic_slice.19
  76.9 0.6 dynamic_slice.18
  77.5 0.0 copy-done.9
  77.5 0.1 reshape.95
  77.6 0.1 pad.9
  77.7 0.6 pad_add_fusion.length_ref
  78.4 0.1 fusion.25.weave_ref
  78.5 14.6 %all-gather.2.cloned.1.call-done = bf16[12288,128]{1,0:T(8,128)(2,1)} async-done(((bf16[384,128]{1,0:T(8,128)(2,1)}), bf16[12288,128]{1,0:T(8,128)(2,1)}) %all-gather.2.cloned.1.call-update) | async-done | bytes 3145744 | tf_op jit(solution)/shard_map/all_gather | solution.py:347
  93.2 1.0 constant_dynamic-slice_fusion.mel_ref
  94.2 0.0 copy-start.1
  94.2 2.2 %copy-done.1 = bf16[4096,512]{1,0:T(8,128)(2,1)S(1)} copy-done((bf16[4096,512]{1,0:T(8,128)(2,1)S(1)}, bf16[4096,512]{1,0:T(8,128)(2,1)}, u32[]{:S(2)}) %copy-start.1) | copy-done | bytes 4194328
  96.4 21.8 %vocoder.1 = bf16[256,6144]{1,0:T(8,128)(2,1)} custom-call(s32[2]{0:T(128)S(1)} %pad_add_fusion.length_ref, bf16[768,128]{1,0:T(8,128)(2,1)S(1)} %constant_dynamic-slice_fusion.mel_ref, bf16[896,512]{1,0:T(8,128)(2,1)S(1)} %bitcast.47, f32[1,512]{1,0:T(1,128)S(1)} %bitcast.52, bf16[4096,512]{1,0:T(8,128)(2,1)S(1)} %copy-done.1, f32[1,256]{1,0:T(1,128)S(1)} %bitcast.53, ...), custom_call_target="tpu_custom_call" | custom-call | flops 8603566080 | bytes 10000000 | tf_op jit(solution)/shard_map/vocoder/pallas_call | solution.py:249
  (27 shorter events, 0.1 us)
Async XLA Ops:
  6.5 23.0 %copy-start = (f32[100,768]{1,0:T(8,128)S(1)}, f32[100,768]{1,0:T(8,128)}, u32[]{:S(2)}) copy-start(f32[100,768]{1,0:T(8,128)} %param.23) | copy-start | bytes 921604
  6.5 4.7 %copy-start.8 = (bf16[1,768,1024]{2,1,0:T(8,128)(2,1)S(1)}, bf16[1,768,1024]{2,1,0:T(8,128)(2,1)}, u32[]{:S(2)}) copy-start(bf16[1,768,1024]{2,1,0:T(8,128)(2,1)} %param.22) | copy-start | bytes 4718596
  6.5 4.7 %copy-start.15 = (f32[2048]{0:T(1024)S(1)}, f32[2048]{0:T(1024)}, u32[]{:S(2)}) copy-start(f32[2048]{0:T(1024)} %param.26) | copy-start | bytes 24580
  6.5 4.7 %copy-start.16 = (f32[1024]{0:T(1024)S(1)}, f32[1024]{0:T(1024)}, u32[]{:S(2)}) copy-start(f32[1024]{0:T(1024)} %param.28) | copy-start | bytes 12292
  6.5 86.6 %all-gather.2.cloned.1.call-start = ((), (), s32[]{:S(2)}) async-start(), calls=%async_computation | async-start | bytes 3244032 | tf_op jit(solution)/shard_map/all_gather | solution.py:347
  23.7 2.4 %copy-start.14 = (bf16[1024,100]{0,1:T(8,128)(2,1)S(1)}, bf16[1024,100]{0,1:T(8,128)(2,1)}, u32[]{:S(2)}) copy-start(bf16[1024,100]{0,1:T(8,128)(2,1)} %param.29) | copy-start | bytes 614404
  23.7 2.4 %copy-start.17 = (f32[100]{0:T(128)S(1)}, f32[100]{0:T(128)}, u32[]{:S(2)}) copy-start(f32[100]{0:T(128)} %param.30) | copy-start | bytes 1204
  26.1 5.3 %copy-start.10 = (s32[768]{0:T(1024)S(1)}, s32[768]{0:T(1024)}, u32[]{:S(2)}) copy-start(s32[768]{0:T(1024)} %param.42) | copy-start | bytes 9220
  26.1 5.3 %copy-start.11 = (s32[768]{0:T(1024)S(1)}, s32[768]{0:T(1024)}, u32[]{:S(2)}) copy-start(s32[768]{0:T(1024)} %param.41) | copy-start | bytes 9220
  26.2 50.8 %copy-start.18 = (s32[32]{0:T(128)S(1)}, s32[32]{0:T(128)}, u32[]{:S(2)}) copy-start(s32[32]{0:T(128)} %param.43) | copy-start | bytes 388
  26.2 51.4 %copy-start.9 = (bf16[700,512]{1,0:T(8,128)(2,1)S(1)}, bf16[700,512]{1,0:T(8,128)(2,1)}, u32[]{:S(2)}) copy-start(bf16[700,512]{1,0:T(8,128)(2,1)} %param.31) | copy-start | bytes 2150404
  28.9 49.5 %copy-start.12 = (f32[256]{0:T(256)S(1)}, f32[256]{0:T(256)}, u32[]{:S(2)}) copy-start(f32[256]{0:T(256)} %param.35) | copy-start | bytes 3076
  28.9 49.4 %copy-start.13 = (f32[256]{0:T(256)S(1)}, f32[256]{0:T(256)}, u32[]{:S(2)}) copy-start(f32[256]{0:T(256)} %param.38) | copy-start | bytes 3076
  28.9 65.2 %copy-start.2 = (bf16[768,256]{1,0:T(8,128)(2,1)S(1)}, bf16[768,256]{1,0:T(8,128)(2,1)}, u32[]{:S(2)}) copy-start(bf16[768,256]{1,0:T(8,128)(2,1)} %dil_w_ref.1) | copy-start | bytes 1179652
  29.0 65.2 %copy-start.3 = (bf16[768,256]{1,0:T(8,128)(2,1)S(1)}, bf16[768,256]{1,0:T(8,128)(2,1)}, u32[]{:S(2)}) copy-start(bf16[768,256]{1,0:T(8,128)(2,1)} %second_w_ref.1) | copy-start | bytes 1179652
  29.0 65.2 %copy-start.4 = (f32[512]{0:T(512)S(1)}, f32[512]{0:T(512)}, u32[]{:S(2)}) copy-start(f32[512]{0:T(512)} %param.32) | copy-start | bytes 6148
  29.0 65.2 %copy-start.5 = (f32[256]{0:T(256)S(1)}, f32[256]{0:T(256)}, u32[]{:S(2)}) copy-start(f32[256]{0:T(256)} %param.34) | copy-start | bytes 3076
  29.0 65.2 %copy-start.6 = (f32[256]{0:T(256)S(1)}, f32[256]{0:T(256)}, u32[]{:S(2)}) copy-start(f32[256]{0:T(256)} %param.37) | copy-start | bytes 3076
  29.0 65.2 %copy-start.7 = (f32[256]{0:T(256)S(1)}, f32[256]{0:T(256)}, u32[]{:S(2)}) copy-start(f32[256]{0:T(256)} %param.40) | copy-start | bytes 3076
  29.0 1.6 %collective-permute-start = (f32[384,100]{1,0:T(8,128)S(1)}, f32[384,100]{1,0:T(8,128)S(1)}, u32[]{:S(2)}, u32[]{:S(2)}) collective-permute-start(f32[384,100]{1,0:T(8,128)S(1)} %constant_dynamic-slice_fusion.1), channel_id=1, source_target_pairs={{0,16},{16,0},{1,17},{17,1},{2,18},{18,2},{3,19},{19,3},{4,20},{20... | collective-permute-start | bytes 460808 | tf_op jit(solution)/shard_map/ppermute | solution.py:43
  94.2 2.2 %copy-start.1 = (bf16[4096,512]{1,0:T(8,128)(2,1)S(1)}, bf16[4096,512]{1,0:T(8,128)(2,1)}, u32[]{:S(2)}) copy-start(bf16[4096,512]{1,0:T(8,128)(2,1)} %up_w_ref.1) | copy-start | bytes 12582916
Sparse Core Ops, SparseCore 0:
  31.5 61.6 all-gather.1

commit v2 on v1

--- a/solution.py
+++ b/solution.py
@@ -1,3 +1,4 @@
+import functools
 import math
 
 import jax
@@ -284,13 +285,120 @@
     )
 
 
-def begins(frame_holder, frame_position, holder_utterance_length):
-    frame_count = frame_holder.shape[0]
-    owners = jnp.arange(holder_utterance_length.shape[0], dtype=jnp.int32)
-    frame = lax.axis_index("seq") * frame_count + jnp.arange(frame_count, dtype=jnp.int32)
-    opens = (frame_holder[:, None] == owners[None, :]) & (frame_position == 0)[:, None]
-    found = jnp.sum(jnp.where(opens, frame[:, None], 0), axis=0)
-    return lax.psum(found.astype(jnp.float32), "seq").astype(jnp.int32)
+def opening_rows(holders, positions):
+    rows = holders.shape[0]
+    frame = jnp.arange(rows, dtype=jnp.int32)[:, None]
+    opens = (holders[:, None] == jnp.arange(LANES, dtype=jnp.int32)) & (positions == 0)[:, None]
+    any_open = jnp.sum(opens.astype(jnp.int32), axis=0)
+    place = jnp.sum(jnp.where(opens, frame, 0), axis=0)
+    tags = jnp.stack([any_open, place // LANES, place % LANES]).astype(jnp.bfloat16)
+    return jnp.pad(tags, ((0, 13), (0, 0)))
+
+
+def gather_kernel(lines, block_ref, out_ref, *sems):
+    line_sem, x_sem, y_sem, fx_sem, fy_sem, core_sem = (sems[2 * i : 2 * i + 2] for i in range(6))
+    branch = lax.axis_index("branch")
+    seq = lax.axis_index("seq")
+    line, y, x = seq // 4, lax.rem(seq, 4) // 2, lax.rem(seq, 2)
+    rows = block_ref.shape[0]
+    half = rows // 32 * 16
+
+    def at(line_, y_, x_):
+        return line_ * 4 + y_ * 2 + x_
+
+    x_side, y_side = (branch, at(line, y, 1 - x)), (branch, at(line, 1 - y, x))
+    core_side = (1 - branch, seq)
+    along = [(branch, at(lax.rem(line + d, lines), y, x)) for d in range(lines)]
+
+    barrier = pltpu.get_barrier_semaphore()
+    partners = along[1:] + [x_side, y_side, core_side]
+    for device in partners:
+        pl.semaphore_signal(barrier, inc=1, device_id=device, device_id_type=pl.DeviceIdType.MESH)
+    out_ref[seq * 2 + branch] = block_ref[...]
+    pl.semaphore_wait(barrier, len(partners))
+
+    started = []
+
+    def send(index, start, size, device, pair, slot):
+        piece = out_ref.at[index, pl.ds(start, size)]
+        copy = pltpu.make_async_remote_copy(
+            src_ref=piece,
+            dst_ref=piece,
+            send_sem=pair[0].at[slot],
+            recv_sem=pair[1].at[slot],
+            device_id=device,
+            device_id_type=pl.DeviceIdType.MESH,
+        )
+        copy.start()
+        started.append(copy)
+
+    def arrived(index, start, size, device, pair, slot):
+        piece = out_ref.at[index, pl.ds(start, size)]
+        pltpu.make_async_remote_copy(
+            src_ref=piece,
+            dst_ref=piece,
+            send_sem=pair[0].at[slot],
+            recv_sem=pair[1].at[slot],
+            device_id=device,
+            device_id_type=pl.DeviceIdType.MESH,
+        ).wait_recv()
+
+    def block_of(d, y_, x_, side=branch):
+        return at(lax.rem(line - d + lines, lines), y_, x_) * 2 + side
+
+    def forward(d):
+        over_x, over_y = block_of(d, y, 1 - x), block_of(d, 1 - y, x)
+        arrived(over_x, 0, rows, x_side, x_sem, d)
+        send(over_x, 0, half, y_side, fy_sem, d)
+        arrived(over_y, 0, rows, y_side, y_sem, d)
+        send(over_y, half, rows - half, x_side, fx_sem, d)
+        send(over_x, 0, rows, core_side, core_sem, 4 * d + 1)
+        send(over_y, 0, rows, core_side, core_sem, 4 * d + 2)
+
+    def finish(d):
+        corner = block_of(d, 1 - y, 1 - x)
+        arrived(corner, 0, half, y_side, fy_sem, d)
+        arrived(corner, half, rows - half, x_side, fx_sem, d)
+        send(corner, 0, rows, core_side, core_sem, 4 * d + 3)
+
+    for d in range(1, lines):
+        send(seq * 2 + branch, 0, rows, along[d], line_sem, d)
+    for d in range(lines):
+        mine = block_of(d, y, x)
+        if d:
+            arrived(mine, 0, rows, along[d], line_sem, d)
+        send(mine, 0, rows, x_side, x_sem, d)
+        send(mine, 0, rows, y_side, y_sem, d)
+        send(mine, 0, rows, core_side, core_sem, 4 * d)
+        if d:
+            forward(d - 1)
+    forward(lines - 1)
+    for d in range(lines):
+        finish(d)
+    for d in range(lines):
+        for slot, (y_, x_) in enumerate(((y, x), (y, 1 - x), (1 - y, x), (1 - y, 1 - x))):
+            arrived(block_of(d, y_, x_, 1 - branch), 0, rows, core_side, core_sem, 4 * d + slot)
+    for copy in started:
+        copy.wait_send()
+
+
+def gather_blocks(block):
+    seq_count = lax.axis_size("seq")
+    lines = seq_count // 4
+    dma = pltpu.SemaphoreType.DMA
+    counts = (lines, lines, lines, lines, lines, 4 * lines)
+    vmem = pl.BlockSpec(memory_space=pltpu.VMEM)
+    return pl.pallas_call(
+        functools.partial(gather_kernel, lines),
+        out_shape=jax.ShapeDtypeStruct((2 * seq_count,) + block.shape, block.dtype),
+        in_specs=[vmem],
+        out_specs=vmem,
+        scratch_shapes=[dma((count,)) for count in counts for _ in range(2)],
+        compiler_params=pltpu.CompilerParams(
+            collective_id=0, has_side_effects=True, vmem_limit_bytes=24 * 1024 * 1024
+        ),
+        name="gather_blocks",
+    )(block)
 
 
 def local(
@@ -340,14 +448,24 @@
     noisy_half = lax.dynamic_slice_in_dim(noisy_mel_state, branch_side * half_rows, half_rows, 1)
     refined = (noisy_half.T + step_size * guided).astype(jnp.bfloat16)
     refined = jnp.pad(refined, ((0, 0), (0, -mel_bins % LANES)))
+    holders = lax.dynamic_slice_in_dim(frame_holder, branch_side * half_rows, half_rows, 0)
+    positions = lax.dynamic_slice_in_dim(frame_position, branch_side * half_rows, half_rows, 0)
+    block = jnp.concatenate([refined, opening_rows(holders, positions)], axis=0)
 
     self_owner = lax.axis_index(("branch", "seq"))
-    utterance_frames_length = holder_utterance_length[self_owner]
-    begin = begins(frame_holder, frame_position, holder_utterance_length)[self_owner]
-    frames = lax.all_gather(refined, ("seq", "branch"), axis=0, tiled=True)
-    first = jnp.minimum(begin, frames.shape[0] - frame_count)
-    holder_mel = lax.dynamic_slice_in_dim(frames, first, frame_count, 0)
-    utterance_frames_length = jnp.stack([utterance_frames_length, begin - first])
+    length = holder_utterance_length[self_owner]
+    blocks = gather_blocks(block)
+    block_count = blocks.shape[0]
+    tags = lax.dynamic_slice(blocks, (0, half_rows, self_owner), (block_count, 3, 1))
+    tags = tags[:, :, 0].astype(jnp.float32)
+    places = jnp.arange(block_count, dtype=jnp.float32) * half_rows
+    begin = jnp.sum(tags[:, 0] * (places + LANES * tags[:, 1] + tags[:, 2])).astype(jnp.int32)
+    low = jnp.minimum(begin // half_rows, block_count - 3)
+    near = lax.dynamic_slice(blocks, (low, 0, 0), (3, half_rows, LANES)).reshape(-1, LANES)
+    begin = begin - low * half_rows
+    first = jnp.minimum(begin, near.shape[0] - frame_count)
+    holder_mel = lax.dynamic_slice_in_dim(near, first, frame_count, 0)
+    utterance_frames_length = jnp.stack([length, begin - first])
     wave = vocoder_synthesize(
         holder_mel,
         utterance_frames_length,

time: 125 us -> 82.1 us (0.66)
  blocking collectives: 43.6 us -> 0 us
  Pallas kernels: 21.8 us -> 48.6 us
  waiting for transfers between devices: 15.6 us -> 0.01 us
  between operations: 14.9 us -> 1.08 us
  local copies, waits for them, and re-layouts: 5.44 us -> 8.44 us
    psum x1 -> x0, blocking collectives: 43.6 us -> none  [begins(): return lax.psum(found.astype(jnp.float32), 'seq').astype(jnp.int32)]
    pallas_call x0 -> x1, Pallas kernels: none -> 26.6 us  [gather_blocks(): pl.pallas_call(functools.partial(gather_kernel, lines), out_shape=jax.Sha...]
    all_gather x1 -> x0, waiting for transfers between devices: 14.6 us -> none  [local(): frames = lax.all_gather(refined, ('seq', 'branch'), axis=0, tiled=True)]
    unnamed x39 -> x43, local copies, waits for them, and re-layouts: 2.41 us -> 5.1 us
    reshape x1, local copies, waits for them, and re-layouts: 0.11 us -> 1.43 us  [vocoder_synthesize(): pre_weight = input_conv_weight.reshape(KPRE, bins, hidden_channels)]
  transfers between devices with their start and end apart: 2 -> 1, of which waited for: 2 -> 0; matrix products, arithmetic and copies ran while one was open for 2% -> 3% of each run, Pallas kernels for 0% -> 0%
where the time goes in v2:
time: 82.1 us; the launch traced here: 81.8 us
  Pallas kernels  48.6 us (59%)
  matrix products  14.2 us (17%)
  other arithmetic  8.97 us (11%)
  local copies, waits for them, and re-layouts  8.44 us (10%)
  between operations  1.08 us (1%)
    pallas_call x1, Pallas kernels, gather_blocks(): pl.pallas_call(functools.partial(gather_kernel, lines), out_shape=jax.Sha...  26.6 us
    pallas_call x1, Pallas kernels, vocoder_synthesize(): pl.pallas_call(vocoder_kernel, out_shape=jax.ShapeDtypeStruct((channels,...  21.9 us
    dot_general x1, matrix products, velocity(): jnp.dot(active, feedforward_out_weight, preferred_element_type=jnp.float32)  12.4 us
    unnamed x43, local copies, waits for them, and re-layouts  5.1 us
    reduce_sum x2, other arithmetic, layer_norm(): row_var = jnp.mean(centred * centred, axis=-1, keepdims=True)  4.45 us
    dot_general x1, matrix products, velocity(): jnp.dot(final_norm, mel_velocity_weight, preferred_element_type=jnp.float32)  1.75 us
    reduce_sum x1, other arithmetic, layer_norm(): row_mean = jnp.mean(row_block, axis=-1, keepdims=True)  1.68 us
  transfers between devices with their start and end apart: 1, of which 0 were waited for; matrix products, arithmetic and copies ran while one was open for 3% of the time, Pallas kernels for 0%

profile of v2, /device:TPU:0, one launch (start us, length us, event | category | flops | bytes accessed | tf_op | source)
XLA Modules:
  0.0 81.8 jit_solution(10359099824869834134)
XLA Ops:
  0.0 1.0 %slice_add_fusion = (f32[1,1024]{1,0:T(1,128)S(1)}, f32[1,1024]{1,0:T(1,128)S(1)}, f32[1,1024]{1,0:T(1,128)S(1)}, f32[1,1024]{1,0:T(1,128)S(1)}, f32[1,1024]{1,0:T(1,128)S(1)}) fusion(f32[5,1024]{1,0:T(8,128)} %param.24), kind=kLoop, calls=%fused_computation.45 | loop fusion | flops 2048 | bytes 40960 | tf_op jit(solution)/shard_map/add | solution.py:76
  1.0 1.7 %convert_reduce_fusion = f32[768]{0:T(1024)S(1)} fusion(bf16[1,768,1024]{2,1,0:T(8,128)(2,1)} %param.22), kind=kLoop, calls=%fused_computation.9 | loop fusion | flops 1572096 | bytes 1575936 | tf_op jit(solution)/shard_map/reduce_sum | solution.py:48
  2.7 2.0 %fusion.12 = f32[768]{0:T(1024)S(1)} fusion(bf16[1,768,1024]{2,1,0:T(8,128)(2,1)} %param.22, f32[768]{0:T(1024)S(1)} %broadcast_multiply_fusion.1), kind=kLoop, calls=%fused_computation.15 | loop fusion | flops 3144960 | bytes 1579008 | tf_op jit(solution)/shard_map/reduce_sum | solution.py:50
  4.7 0.0 copy-done.9
  4.7 0.0 copy-done.17
  4.7 0.0 copy-done.18
  4.7 12.4 %fusion.47 = (f32[768]{0:T(1024)S(1)}, f32[768,1024]{1,0:T(8,128)}) fusion(f32[1024]{0:T(1024)S(1)} %copy-done.18, bf16[2048,1024]{1,0:T(8,128)(2,1)} %param.27, bf16[1024,2048]{1,0:T(8,128)(2,1)} %param.25, f32[2048]{0:T(1024)S(1)} %copy-done.17, bf16[1,768,1024]{2,1,0:T(8,128)(2,1)S(1)} %copy-done.9, f32[1024]{0:T(1024)S(1)} %bitcast.92, ...), kind=kOutput, calls=%fused_computation.87 | convolution fusion | flops 6466829312 | bytes 13140992 | tf_op jit(solution)/shard_map/dot_general | solution.py:72
  17.1 2.5 %multiply_reduce_fusion = f32[768]{0:T(1024)S(1)} fusion(f32[768,1024]{1,0:T(8,128)} %get-tuple-element.19, f32[768]{0:T(1024)S(1)} %broadcast_multiply_fusion), kind=kLoop, calls=%fused_computation.20 | loop fusion | flops 2358528 | bytes 3151872 | tf_op jit(solution)/shard_map/reduce_sum | solution.py:50
  19.6 0.0 copy-start.16
  19.6 0.0 copy-start.15
  19.6 0.0 copy-start.13
  19.7 0.0 copy-start.14
  19.7 0.3 copy-done.10
  20.0 0.0 copy-done.19
  20.0 1.8 %fusion.22 = f32[768,100]{1,0:T(8,128)S(1)} fusion(bf16[1024,100]{0,1:T(8,128)(2,1)} %param.29, f32[768,1024]{1,0:T(8,128)S(1)} %copy-done.10, f32[1024]{0:T(1024)S(1)} %bitcast.91, f32[1024]{0:T(1024)S(1)} %bitcast.90, f32[768]{0:T(1024)S(1)} %add_rsqrt_fusion, f32[768]{0:T(1024)S(1)} %broadcast_multiply_fusion, f32[100]{0:T(128)S(1)} %copy-done.19), kind=kOutput, calls=%fused_computation.26 | convolution fusion | flops 161295360 | bytes 3672464 | tf_op jit(solution)/shard_map/dot_general | solution.py:79
  21.7 0.0 copy-start.11
  21.7 0.7 copy-done.11
  22.5 0.0 copy-start.12
  22.5 0.5 collective-permute-start
  23.0 0.0 copy-done.16
  23.0 0.1 dynamic_slice.31
  23.1 0.0 copy-done.15
  23.1 0.1 dynamic-slice_compare_fusion
  23.2 0.2 convert_reduce_fusion.1
  23.5 0.1 fusion.25.weave_ref
  23.6 0.1 copy.33
  23.8 1.4 %reshape.171 = bf16[7,100,512]{2,1,0:T(8,128)(2,1)S(1)} reshape(bf16[700,512]{1,0:T(8,128)(2,1)} %param.31) | data formatting | bytes 1433600 | tf_op jit(solution)/shard_map/reshape | solution.py:243
  25.2 0.6 dynamic_slice.27
  25.8 0.1 pad.14
  25.9 0.0 copy-start.3
  25.9 0.0 copy-start.4
  25.9 0.0 copy-start.5
  25.9 0.0 copy-start.6
  25.9 0.0 copy-start.7
  25.9 0.0 copy-start.8
  26.0 0.0 collective-permute-done
  26.0 0.1 fusion.27
  26.1 26.6 %gather_blocks.1 = bf16[32,400,128]{2,1,0:T(8,128)(2,1)S(1)} custom-call(bf16[400,128]{1,0:T(8,128)(2,1)S(1)} %fusion.29.block_ref), custom_call_target="tpu_custom_call" | custom-call | tf_op jit(solution)/shard_map/gather_blocks/pallas_call | solution.py:391
  52.7 1.7 %copy-done.1 = bf16[32,400,128]{2,1,0:T(8,128)(2,1)} copy-done((bf16[32,400,128]{2,1,0:T(8,128)(2,1)}, bf16[32,400,128]{2,1,0:T(8,128)(2,1)S(1)}, u32[]{:S(2)}) %copy-start.1) | copy-done | bytes 3276824
  54.4 0.1 dynamic-slice_convert_fusion
  54.5 0.1 copy.31
  54.6 0.6 fusion.41
  55.9 1.0 %constant_dynamic-slice_fusion.1 = bf16[3,384,128]{2,1,0:T(8,128)(2,1)S(1)} fusion(bf16[32,400,128]{2,1,0:T(8,128)(2,1)} %copy-done.1, s32[]{:T(128)S(6)} %select_n.99), kind=kLoop, calls=%fused_computation.62 | loop fusion | bytes 589828 | tf_op jit(solution)/shard_map/dynamic_slice | solution.py:464
  56.9 0.1 constant_dynamic-slice_fusion.mel_ref
  57.0 0.6 pad_add_fusion.length_ref
  57.6 0.0 copy-start.2
  57.7 2.2 %copy-done.2 = bf16[4096,512]{1,0:T(8,128)(2,1)S(1)} copy-done((bf16[4096,512]{1,0:T(8,128)(2,1)S(1)}, bf16[4096,512]{1,0:T(8,128)(2,1)}, u32[]{:S(2)}) %copy-start.2) | copy-done | bytes 4194328
  59.8 21.9 %vocoder.1 = bf16[256,6144]{1,0:T(8,128)(2,1)} custom-call(s32[2]{0:T(128)S(1)} %pad_add_fusion.length_ref, bf16[768,128]{1,0:T(8,128)(2,1)S(1)} %constant_dynamic-slice_fusion.mel_ref, bf16[896,512]{1,0:T(8,128)(2,1)S(1)} %bitcast.79, f32[1,512]{1,0:T(1,128)S(1)} %bitcast.84, bf16[4096,512]{1,0:T(8,128)(2,1)S(1)} %copy-done.2, f32[1,256]{1,0:T(1,128)S(1)} %bitcast.85, ...), custom_call_target="tpu_custom_call" | custom-call | flops 8603566080 | bytes 10000000 | tf_op jit(solution)/shard_map/vocoder/pallas_call | solution.py:250
  (32 shorter events, 0.2 us)
Async XLA Ops:
  0.0 23.6 %copy-start = (f32[100,768]{1,0:T(8,128)S(1)}, f32[100,768]{1,0:T(8,128)}, u32[]{:S(2)}) copy-start(f32[100,768]{1,0:T(8,128)} %param.23) | copy-start | bytes 921604
  0.0 4.7 %copy-start.9 = (bf16[1,768,1024]{2,1,0:T(8,128)(2,1)S(1)}, bf16[1,768,1024]{2,1,0:T(8,128)(2,1)}, u32[]{:S(2)}) copy-start(bf16[1,768,1024]{2,1,0:T(8,128)(2,1)} %param.22) | copy-start | bytes 4718596
  0.0 4.7 %copy-start.17 = (f32[2048]{0:T(1024)S(1)}, f32[2048]{0:T(1024)}, u32[]{:S(2)}) copy-start(f32[2048]{0:T(1024)} %param.26) | copy-start | bytes 24580
  0.0 4.7 %copy-start.18 = (f32[1024]{0:T(1024)S(1)}, f32[1024]{0:T(1024)}, u32[]{:S(2)}) copy-start(f32[1024]{0:T(1024)} %param.28) | copy-start | bytes 12292
  17.1 2.8 %copy-start.10 = (f32[768,1024]{1,0:T(8,128)S(1)}, f32[768,1024]{1,0:T(8,128)}, u32[]{:S(2)}) copy-start(f32[768,1024]{1,0:T(8,128)} %get-tuple-element.19) | copy-start | bytes 9437188
  17.1 2.8 %copy-start.19 = (f32[100]{0:T(128)S(1)}, f32[100]{0:T(128)}, u32[]{:S(2)}) copy-start(f32[100]{0:T(128)} %param.30) | copy-start | bytes 1204
  19.6 3.4 %copy-start.16 = (s32[768]{0:T(1024)S(1)}, s32[768]{0:T(1024)}, u32[]{:S(2)}) copy-start(s32[768]{0:T(1024)} %param.41) | copy-start | bytes 9220
  19.6 3.5 %copy-start.15 = (s32[768]{0:T(1024)S(1)}, s32[768]{0:T(1024)}, u32[]{:S(2)}) copy-start(s32[768]{0:T(1024)} %param.42) | copy-start | bytes 9220
  19.6 3.8 %copy-start.13 = (f32[256]{0:T(256)S(1)}, f32[256]{0:T(256)}, u32[]{:S(2)}) copy-start(f32[256]{0:T(256)} %param.35) | copy-start | bytes 3076
  19.7 3.8 %copy-start.14 = (f32[256]{0:T(256)S(1)}, f32[256]{0:T(256)}, u32[]{:S(2)}) copy-start(f32[256]{0:T(256)} %param.38) | copy-start | bytes 3076
  20.0 5.2 %copy-start.20 = (s32[32]{0:T(128)S(1)}, s32[32]{0:T(128)}, u32[]{:S(2)}) copy-start(s32[32]{0:T(128)} %param.43) | copy-start | bytes 388
  21.7 0.7 copy-start.11
  22.5 3.5 %copy-start.12 = (f32[768,100]{1,0:T(8,128)S(1)}, f32[768,100]{1,0:T(8,128)}, u32[]{:S(2)}) copy-start(f32[768,100]{1,0:T(8,128)} %copy-done.11) | copy-start | bytes 921604
  22.5 3.5 %collective-permute-start = (f32[384,100]{1,0:T(8,128)S(1)}, f32[384,100]{1,0:T(8,128)S(1)}, u32[]{:S(2)}, u32[]{:S(2)}) collective-permute-start(f32[384,100]{1,0:T(8,128)S(1)} %constant_dynamic-slice_fusion.2), channel_id=1, source_target_pairs={{0,16},{16,0},{1,17},{17,1},{2,18},{18,2},{3,19},{19,3},{4,20},{20... | collective-permute-start | bytes 460808 | tf_op jit(solution)/shard_map/ppermute | solution.py:44
  25.9 31.7 %copy-start.3 = (bf16[768,256]{1,0:T(8,128)(2,1)S(1)}, bf16[768,256]{1,0:T(8,128)(2,1)}, u32[]{:S(2)}) copy-start(bf16[768,256]{1,0:T(8,128)(2,1)} %dil_w_ref.1) | copy-start | bytes 1179652
  25.9 31.7 %copy-start.4 = (bf16[768,256]{1,0:T(8,128)(2,1)S(1)}, bf16[768,256]{1,0:T(8,128)(2,1)}, u32[]{:S(2)}) copy-start(bf16[768,256]{1,0:T(8,128)(2,1)} %second_w_ref.1) | copy-start | bytes 1179652
  25.9 31.7 %copy-start.5 = (f32[512]{0:T(512)S(1)}, f32[512]{0:T(512)}, u32[]{:S(2)}) copy-start(f32[512]{0:T(512)} %param.32) | copy-start | bytes 6148
  25.9 31.7 %copy-start.6 = (f32[256]{0:T(256)S(1)}, f32[256]{0:T(256)}, u32[]{:S(2)}) copy-start(f32[256]{0:T(256)} %param.34) | copy-start | bytes 3076
  25.9 31.7 %copy-start.7 = (f32[256]{0:T(256)S(1)}, f32[256]{0:T(256)}, u32[]{:S(2)}) copy-start(f32[256]{0:T(256)} %param.37) | copy-start | bytes 3076
  25.9 31.7 %copy-start.8 = (f32[256]{0:T(256)S(1)}, f32[256]{0:T(256)}, u32[]{:S(2)}) copy-start(f32[256]{0:T(256)} %param.40) | copy-start | bytes 3076
  52.7 1.7 %copy-start.1 = (bf16[32,400,128]{2,1,0:T(8,128)(2,1)}, bf16[32,400,128]{2,1,0:T(8,128)(2,1)S(1)}, u32[]{:S(2)}) copy-start(bf16[32,400,128]{2,1,0:T(8,128)(2,1)S(1)} %gather_blocks.1) | copy-start | bytes 9830404
  57.6 2.2 %copy-start.2 = (bf16[4096,512]{1,0:T(8,128)(2,1)S(1)}, bf16[4096,512]{1,0:T(8,128)(2,1)}, u32[]{:S(2)}) copy-start(bf16[4096,512]{1,0:T(8,128)(2,1)} %up_w_ref.1) | copy-start | bytes 12582916

commit v3 on v2

--- a/solution.py
+++ b/solution.py
@@ -51,6 +51,37 @@
     return centred * lax.rsqrt(row_var + 1e-06)
 
 
+def velocity_kernel(
+    rows_ref, mod_ref, in_w_ref, in_b_ref, out_w_ref, out_b_ref, mel_w_ref, mel_b_ref, out_ref,
+    normed, total,
+):
+    step = pl.program_id(0)
+    chunk = math.gcd(rows_ref.shape[0], CHUNK)
+    pieces = [pl.ds(i * chunk, chunk) for i in range(rows_ref.shape[0] // chunk)]
+    modulation = [mod_ref[i : i + 1] for i in range(5)]
+
+    @pl.when(step == 0)
+    def _():
+        for piece in pieces:
+            plain = layer_norm(rows_ref[piece].astype(jnp.float32))
+            normed[piece] = (plain * (1.0 + modulation[1]) + modulation[0]).astype(jnp.bfloat16)
+            total[piece] = jnp.zeros((chunk, total.shape[1]), jnp.float32)
+
+    for piece in pieces:
+        inner = product(normed[piece], in_w_ref[...], 1, 0) + in_b_ref[...]
+        bend = inner * (math.sqrt(2.0 / math.pi) * (1.0 + 0.044715 * inner * inner))
+        active = (0.5 * inner * (1.0 + jnp.tanh(bend))).astype(jnp.bfloat16)
+        total[piece] += product(active, out_w_ref[...], 1, 0)
+
+    @pl.when(step == pl.num_programs(0) - 1)
+    def _():
+        for piece in pieces:
+            back = modulation[2] * (total[piece] + out_b_ref[...])
+            plain = layer_norm(rows_ref[piece].astype(jnp.float32) + back)
+            final = (plain * (1.0 + modulation[4]) + modulation[3]).astype(jnp.bfloat16)
+            out_ref[piece] = product(final, mel_w_ref[...], 1, 0) + mel_b_ref[...]
+
+
 def velocity(
     row_block,
     modulation,
@@ -61,23 +92,51 @@
     mel_velocity_weight,
     mel_velocity_bias,
 ):
-    residual_in = row_block.astype(jnp.float32)
-    normed = (layer_norm(residual_in) * (1.0 + modulation[1]) + modulation[0]).astype(jnp.bfloat16)
-    inner_pre = (
-        jnp.dot(normed, feedforward_in_weight, preferred_element_type=jnp.float32)
-        + feedforward_in_bias
-    )
-    active = jax.nn.gelu(inner_pre, approximate=True).astype(jnp.bfloat16)
-    back_proj = (
-        jnp.dot(active, feedforward_out_weight, preferred_element_type=jnp.float32)
-        + feedforward_out_bias
-    )
-    block_out = residual_in + modulation[2] * back_proj
-    final_norm = (layer_norm(block_out) * (1.0 + modulation[4]) + modulation[3]).astype(
-        jnp.bfloat16
-    )
-    speed = jnp.dot(final_norm, mel_velocity_weight, preferred_element_type=jnp.float32)
-    return speed + mel_velocity_bias
+    rows, width = row_block.shape
+    inner = feedforward_in_weight.shape[1]
+    part = math.gcd(inner, 512)
+    spare = -mel_velocity_weight.shape[1] % LANES
+    mel_weight = jnp.pad(mel_velocity_weight, ((0, 0), (0, spare)))
+    mel_bias = jnp.pad(mel_velocity_bias, (0, spare))
+
+    def whole(*shape):
+        return pl.BlockSpec(shape, lambda i: (0,) * len(shape))
+
+    lanes = mel_weight.shape[1]
+    return pl.pallas_call(
+        velocity_kernel,
+        grid=(inner // part,),
+        out_shape=jax.ShapeDtypeStruct((rows, lanes), jnp.float32),
+        in_specs=[
+            whole(rows, width),
+            whole(5, width),
+            pl.BlockSpec((width, part), lambda i: (0, i)),
+            pl.BlockSpec((1, part), lambda i: (0, i)),
+            pl.BlockSpec((part, width), lambda i: (i, 0)),
+            whole(1, width),
+            whole(width, lanes),
+            whole(1, lanes),
+        ],
+        out_specs=whole(rows, lanes),
+        scratch_shapes=[
+            pltpu.VMEM((rows, width), jnp.bfloat16),
+            pltpu.VMEM((rows, width), jnp.float32),
+        ],
+        compiler_params=pltpu.CompilerParams(vmem_limit_bytes=32 * 1024 * 1024),
+        cost_estimate=pl.CostEstimate(
+            flops=4 * rows * width * inner, bytes_accessed=11_000_000, transcendentals=rows * inner
+        ),
+        name="velocity",
+    )(
+        row_block,
+        modulation,
+        feedforward_in_weight,
+        feedforward_in_bias[None],
+        feedforward_out_weight,
+        feedforward_out_bias[None],
+        mel_weight,
+        mel_bias[None],
+    )
 
 
 def snake(signal, turns, inverse):
@@ -436,7 +495,7 @@
         mel_velocity_weight,
         mel_velocity_bias,
     )
-    frame_count, mel_bins = own_velocity.shape
+    frame_count, lanes = own_velocity.shape
     half_rows = frame_count // 2
     branch_side = lax.axis_index("branch")
     own_half = lax.dynamic_slice_in_dim(own_velocity, branch_side * half_rows, half_rows, 0)
@@ -446,8 +505,8 @@
     unconditional = jnp.where(branch_side == 0, peer_half, own_half)
     guided = (1.0 + GUIDE) * conditional - GUIDE * unconditional
     noisy_half = lax.dynamic_slice_in_dim(noisy_mel_state, branch_side * half_rows, half_rows, 1)
+    noisy_half = jnp.pad(noisy_half, ((0, lanes - noisy_half.shape[0]), (0, 0)))
     refined = (noisy_half.T + step_size * guided).astype(jnp.bfloat16)
-    refined = jnp.pad(refined, ((0, 0), (0, -mel_bins % LANES)))
     holders = lax.dynamic_slice_in_dim(frame_holder, branch_side * half_rows, half_rows, 0)
     positions = lax.dynamic_slice_in_dim(frame_position, branch_side * half_rows, half_rows, 0)
     block = jnp.concatenate([refined, opening_rows(holders, positions)], axis=0)

time: 82.1 us -> 82.5 us (level)
  matrix products: 14.2 us -> 0 us
  Pallas kernels: 48.6 us -> 61.3 us
  local copies, waits for them, and re-layouts: 8.44 us -> 16.5 us
  other arithmetic: 8.97 us -> 2.75 us
    dot_general x2 -> x0, matrix products: 14.2 us -> none  [the longest x1 12.4 us: velocity(): jnp.dot(active, feedforward_out_weight, preferred_element_type=jnp.float32)]
    pallas_call x0 -> x1, Pallas kernels: none -> 12.8 us  [velocity(): pl.pallas_call(velocity_kernel, grid=(inner // part,), out_shape=jax.Shap...]
    unnamed x43 -> x44, local copies, waits for them, and re-layouts: 5.1 us -> 13.1 us
    reduce_sum x3 -> x0, other arithmetic: 6.13 us -> none  [the longest x2 4.45 us: layer_norm(): row_var = jnp.mean(centred * centred, axis=-1, keepdims=True)]
    reshape x1, local copies, waits for them, and re-layouts: 1.43 us -> 0.11 us  [vocoder_synthesize(): pre_weight = input_conv_weight.reshape(KPRE, bins, hidden_channels)]
    add x1 -> x0, other arithmetic: 0.98 us -> none  [velocity(): 1.0 + modulation[4]]
    convert_element_type x1, other arithmetic: 0.07 us -> 1.01 us  [local(): refined = (noisy_half.T + step_size * guided).astype(jnp.bfloat16)]
  transfers between devices with their start and end apart: 1 -> 1, of which waited for: 0 -> 0; matrix products, arithmetic and copies ran while one was open for 3% -> 2% of each run, Pallas kernels for 0% -> 0%
where the time goes in v3:
time: 82.5 us; the launch traced here: 82 us
  Pallas kernels  61.3 us (74%)
  local copies, waits for them, and re-layouts  16.5 us (20%)
  other arithmetic  2.75 us (3%)
  between operations  0.99 us (1%)
    pallas_call x1, Pallas kernels, gather_blocks(): pl.pallas_call(functools.partial(gather_kernel, lines), out_shape=jax.Sha...  26.6 us
    pallas_call x1, Pallas kernels, vocoder_synthesize(): pl.pallas_call(vocoder_kernel, out_shape=jax.ShapeDtypeStruct((channels,...  21.8 us
    unnamed x44, local copies, waits for them, and re-layouts  13.1 us
    pallas_call x1, Pallas kernels, velocity(): pl.pallas_call(velocity_kernel, grid=(inner // part,), out_shape=jax.Shap...  12.8 us
  transfers between devices with their start and end apart: 1, of which 0 were waited for; matrix products, arithmetic and copies ran while one was open for 2% of the time, Pallas kernels for 0%

profile of v3, /device:TPU:0, one launch (start us, length us, event | category | flops | bytes accessed | tf_op | source)
XLA Modules:
  0.0 82.0 jit_solution(16438063821550916946)
XLA Ops:
  0.0 0.0 copy-start
  0.0 1.2 %copy.30 = bf16[1024,100]{1,0:T(8,128)(2,1)S(1)} copy(bf16[1024,100]{0,1:T(8,128)(2,1)} %param.29) | data formatting | bytes 409600 | tf_op args[7]
  1.2 0.7 pad_bitcast_fusion.mel_b_ref
  1.8 0.1 pad.21.mel_w_ref
  1.9 0.0 copy-start.2
  1.9 2.2 %copy-done.2 = bf16[1024,2048]{1,0:T(8,128)(2,1)S(1)} copy-done((bf16[1024,2048]{1,0:T(8,128)(2,1)S(1)}, bf16[1024,2048]{1,0:T(8,128)(2,1)}, u32[]{:S(2)}) %copy-start.2) | copy-done | bytes 4194328
  4.1 2.2 %copy-done.3 = bf16[2048,1024]{1,0:T(8,128)(2,1)S(1)} copy-done((bf16[2048,1024]{1,0:T(8,128)(2,1)S(1)}, bf16[2048,1024]{1,0:T(8,128)(2,1)}, u32[]{:S(2)}) %copy-start.3) | copy-done | bytes 4194328
  6.3 1.4 %copy-done.5 = bf16[1,768,1024]{2,1,0:T(8,128)(2,1)S(1)} copy-done((bf16[1,768,1024]{2,1,0:T(8,128)(2,1)S(1)}, bf16[1,768,1024]{2,1,0:T(8,128)(2,1)}, u32[]{:S(2)}) %copy-start.5) | copy-done | bytes 1572888
  7.7 0.8 copy-done.8
  8.4 0.7 copy-done.9
  9.1 0.7 copy-done.10
  9.8 12.8 %velocity.1 = f32[768,128]{1,0:T(8,128)S(1)} custom-call(bf16[768,1024]{1,0:T(8,128)(2,1)S(1)} %bitcast.58, f32[5,1024]{1,0:T(8,128)S(1)} %copy-done.8, bf16[1024,2048]{1,0:T(8,128)(2,1)S(1)} %copy-done.2, f32[1,2048]{1,0:T(1,128)S(1)} %bitcast.59, bf16[2048,1024]{1,0:T(8,128)(2,1)S(1)} %copy-done.3, f32[1,1024]{1,0:T(1,128)S(1)} %bitcast.60, ...), custom_call_target="tpu_custom_call" | custom-call | flops 6442450944 | bytes 11000000 | tf_op jit(solution)/shard_map/velocity/pallas_call | solution.py:106
  22.6 0.0 copy-start.20
  22.6 0.0 copy-start.17
  22.7 0.7 constant_dynamic-slice_fusion.2
  23.4 0.4 collective-permute-start
  23.8 0.0 copy-done.19
  23.8 0.1 dynamic_slice.31
  23.9 0.0 copy-done.18
  23.9 0.1 dynamic-slice_compare_fusion
  24.0 0.2 convert_reduce_fusion
  24.2 0.0 copy-done
  24.2 0.1 copy.32
  24.4 0.1 reshape.143
  24.5 0.0 copy-start.6
  24.5 0.0 copy-start.7
  24.5 0.0 copy-start.11
  24.5 0.0 copy-start.12
  24.6 0.0 copy-start.13
  24.6 0.0 copy-start.14
  24.6 0.1 pad.24
  24.7 0.1 fusion.weave_ref
  24.8 0.0 copy-done.20
  24.8 0.6 dynamic_slice.27
  25.4 0.0 collective-permute-done
  25.4 1.0 %fusion.1 = bf16[384,128]{1,0:T(8,128)(2,1)S(1)} fusion(f32[384,128]{1,0:T(8,128)} %collective-permute-done, f32[768,128]{1,0:T(8,128)S(1)} %velocity.1, s32[]{:T(128)S(6)} %select_n.89, f32[100,384]{0,1:T(8,128)S(1)} %copy.32, pred[]{:T(512)S(6)} %eq.40), kind=kLoop, calls=%fused_computation.3 | loop fusion | flops 393216 | bytes 645125 | tf_op jit(solution)/shard_map/convert_element_type | solution.py:509
  26.4 26.6 %gather_blocks.1 = bf16[32,400,128]{2,1,0:T(8,128)(2,1)S(1)} custom-call(bf16[400,128]{1,0:T(8,128)(2,1)S(1)} %pad_maximum_fusion.block_ref), custom_call_target="tpu_custom_call" | custom-call | tf_op jit(solution)/shard_map/gather_blocks/pallas_call | solution.py:450
  53.1 1.7 %copy-done.1 = bf16[32,400,128]{2,1,0:T(8,128)(2,1)} copy-done((bf16[32,400,128]{2,1,0:T(8,128)(2,1)}, bf16[32,400,128]{2,1,0:T(8,128)(2,1)S(1)}, u32[]{:S(2)}) %copy-start.1) | copy-done | bytes 3276824
  54.7 0.1 dynamic-slice_convert_fusion
  54.8 0.1 copy.31
  54.9 0.6 fusion.14
  56.2 1.0 %constant_dynamic-slice_fusion.1 = bf16[3,384,128]{2,1,0:T(8,128)(2,1)S(1)} fusion(bf16[32,400,128]{2,1,0:T(8,128)(2,1)} %copy-done.1, s32[]{:T(128)S(6)} %select_n.99), kind=kLoop, calls=%fused_computation.27 | loop fusion | bytes 589828 | tf_op jit(solution)/shard_map/dynamic_slice | solution.py:523
  57.2 0.1 constant_dynamic-slice_fusion.mel_ref
  57.3 0.6 pad_add_fusion.length_ref
  57.9 0.0 copy-done.7
  57.9 0.0 copy-start.4
  57.9 2.2 %copy-done.4 = bf16[4096,512]{1,0:T(8,128)(2,1)S(1)} copy-done((bf16[4096,512]{1,0:T(8,128)(2,1)S(1)}, bf16[4096,512]{1,0:T(8,128)(2,1)}, u32[]{:S(2)}) %copy-start.4) | copy-done | bytes 4194328
  60.1 21.8 %vocoder.1 = bf16[256,6144]{1,0:T(8,128)(2,1)} custom-call(s32[2]{0:T(128)S(1)} %pad_add_fusion.length_ref, bf16[768,128]{1,0:T(8,128)(2,1)S(1)} %constant_dynamic-slice_fusion.mel_ref, bf16[896,512]{1,0:T(8,128)(2,1)S(1)} %bitcast.53, f32[1,512]{1,0:T(1,128)S(1)} %bitcast.61, bf16[4096,512]{1,0:T(8,128)(2,1)S(1)} %copy-done.4, f32[1,256]{1,0:T(1,128)S(1)} %bitcast.62, ...), custom_call_target="tpu_custom_call" | custom-call | flops 8603566080 | bytes 10000000 | tf_op jit(solution)/shard_map/vocoder/pallas_call | solution.py:309
  (26 shorter events, 0.1 us)
Async XLA Ops:
  0.0 24.2 %copy-start = (f32[100,768]{1,0:T(8,128)S(1)}, f32[100,768]{1,0:T(8,128)}, u32[]{:S(2)}) copy-start(f32[100,768]{1,0:T(8,128)} %param.23) | copy-start | bytes 921604
  1.9 2.2 %copy-start.2 = (bf16[1024,2048]{1,0:T(8,128)(2,1)S(1)}, bf16[1024,2048]{1,0:T(8,128)(2,1)}, u32[]{:S(2)}) copy-start(bf16[1024,2048]{1,0:T(8,128)(2,1)} %in_w_ref.1) | copy-start | bytes 12582916
  4.1 2.2 %copy-start.3 = (bf16[2048,1024]{1,0:T(8,128)(2,1)S(1)}, bf16[2048,1024]{1,0:T(8,128)(2,1)}, u32[]{:S(2)}) copy-start(bf16[2048,1024]{1,0:T(8,128)(2,1)} %out_w_ref.1) | copy-start | bytes 12582916
  6.3 1.4 %copy-start.5 = (bf16[1,768,1024]{2,1,0:T(8,128)(2,1)S(1)}, bf16[1,768,1024]{2,1,0:T(8,128)(2,1)}, u32[]{:S(2)}) copy-start(bf16[1,768,1024]{2,1,0:T(8,128)(2,1)} %param.22) | copy-start | bytes 4718596
  7.7 0.8 copy-start.8
  8.4 0.7 copy-start.9
  9.1 0.7 copy-start.10
  9.8 14.0 %copy-start.19 = (s32[768]{0:T(1024)S(1)}, s32[768]{0:T(1024)}, u32[]{:S(2)}) copy-start(s32[768]{0:T(1024)} %param.41) | copy-start | bytes 9220
  9.8 14.0 %copy-start.18 = (s32[768]{0:T(1024)S(1)}, s32[768]{0:T(1024)}, u32[]{:S(2)}) copy-start(s32[768]{0:T(1024)} %param.42) | copy-start | bytes 9220
  9.8 14.5 %copy-start.16 = (f32[256]{0:T(256)S(1)}, f32[256]{0:T(256)}, u32[]{:S(2)}) copy-start(f32[256]{0:T(256)} %param.35) | copy-start | bytes 3076
  9.8 14.5 %copy-start.15 = (bf16[700,512]{1,0:T(8,128)(2,1)S(1)}, bf16[700,512]{1,0:T(8,128)(2,1)}, u32[]{:S(2)}) copy-start(bf16[700,512]{1,0:T(8,128)(2,1)} %param.31) | copy-start | bytes 2150404
  22.6 2.1 %copy-start.20 = (s32[32]{0:T(128)S(1)}, s32[32]{0:T(128)}, u32[]{:S(2)}) copy-start(s32[32]{0:T(128)} %param.43) | copy-start | bytes 388
  22.6 2.7 %copy-start.17 = (f32[256]{0:T(256)S(1)}, f32[256]{0:T(256)}, u32[]{:S(2)}) copy-start(f32[256]{0:T(256)} %param.38) | copy-start | bytes 3076
  23.4 2.0 %collective-permute-start = (f32[384,128]{1,0:T(8,128)}, f32[384,128]{1,0:T(8,128)}, u32[]{:S(2)}, u32[]{:S(2)}) collective-permute-start(f32[384,128]{1,0:T(8,128)} %constant_dynamic-slice_fusion.2), channel_id=1, source_target_pairs={{0,16},{16,0},{1,17},{17,1},{2,18},{18,2},{3,19},{19,3},{4,20},{20... | collective-permute-start | bytes 589832 | tf_op jit(solution)/shard_map/ppermute | solution.py:44
  24.5 33.4 %copy-start.6 = (bf16[768,256]{1,0:T(8,128)(2,1)S(1)}, bf16[768,256]{1,0:T(8,128)(2,1)}, u32[]{:S(2)}) copy-start(bf16[768,256]{1,0:T(8,128)(2,1)} %dil_w_ref.1) | copy-start | bytes 1179652
  24.5 33.4 %copy-start.7 = (bf16[768,256]{1,0:T(8,128)(2,1)S(1)}, bf16[768,256]{1,0:T(8,128)(2,1)}, u32[]{:S(2)}) copy-start(bf16[768,256]{1,0:T(8,128)(2,1)} %second_w_ref.1) | copy-start | bytes 1179652
  24.5 33.4 %copy-start.11 = (f32[512]{0:T(512)S(1)}, f32[512]{0:T(512)}, u32[]{:S(2)}) copy-start(f32[512]{0:T(512)} %param.32) | copy-start | bytes 6148
  24.5 33.4 %copy-start.12 = (f32[256]{0:T(256)S(1)}, f32[256]{0:T(256)}, u32[]{:S(2)}) copy-start(f32[256]{0:T(256)} %param.34) | copy-start | bytes 3076
  24.6 33.4 %copy-start.13 = (f32[256]{0:T(256)S(1)}, f32[256]{0:T(256)}, u32[]{:S(2)}) copy-start(f32[256]{0:T(256)} %param.37) | copy-start | bytes 3076
  24.6 33.4 %copy-start.14 = (f32[256]{0:T(256)S(1)}, f32[256]{0:T(256)}, u32[]{:S(2)}) copy-start(f32[256]{0:T(256)} %param.40) | copy-start | bytes 3076
  53.0 1.7 %copy-start.1 = (bf16[32,400,128]{2,1,0:T(8,128)(2,1)}, bf16[32,400,128]{2,1,0:T(8,128)(2,1)S(1)}, u32[]{:S(2)}) copy-start(bf16[32,400,128]{2,1,0:T(8,128)(2,1)S(1)} %gather_blocks.1) | copy-start | bytes 9830404
  57.9 2.2 %copy-start.4 = (bf16[4096,512]{1,0:T(8,128)(2,1)S(1)}, bf16[4096,512]{1,0:T(8,128)(2,1)}, u32[]{:S(2)}) copy-start(bf16[4096,512]{1,0:T(8,128)(2,1)} %up_w_ref.1) | copy-start | bytes 12582916
